TPU v7x, 32 devices: a whole 2x2x4 slice. The times are simulated.
32 devices in a mesh: grid: 8 (over z, y), states: 4 (over x, core).
Axes of the slice: x: 2, y: 2, z: 4, core: 2. Of those that a mesh axis runs over, the one named last changes fastest.
Arguments:
- states_in: float32 [4, 128, 32, 128], P('states', 'grid'), may hold values from -10 to 10
- potential: float32 [128, 32, 128], P('grid'), may hold values from -2 to 0.5
- projectors: bfloat16 [8, 16, 8, 4096], P('grid', 'states'), may hold values from -0.0625 to 0.0625
- proj_gains: bfloat16 [8, 16, 8], P('grid', 'states'), may hold values from 1 to 6
- atom_owner: int32 [80], P('grid'), may hold values from 0 to 7, as said below
- atom_rows: int32 [80, 32], P('grid'), may hold values from -1 to 4095, as said below
- wrap_rows: int32 [32], replicated, may hold values from 0 to 31, as said below
Outputs:
- filtered: float32 [4, 128, 32, 128], P('states', 'grid')
Inputs may be any that keep to these rules, and one draw needn't show every extreme that they name: `atom_owner`: atom a belongs to tile a // 10. At most 2 atoms of one tile share an owner, and one owner takes exactly 2 atoms of every tile. `atom_rows`: A row r is the line of cells at x = r // 32, y = r % 32. Each list holds distinct rows whose x lies in the atom's own tile of 16 planes, followed by -1 entries; each list has 16 rows or more, and the first atom of every tile fills all 32. wrap_rows[y] = (y + t) mod 32 for one t of 1 to 31.
All inputs are finite; a program needn't handle non-finite values.
Results may differ from a plain program's by a relative error of at most 0.00082.
Values may be sent and summed in bfloat16 or wider, within the bound.
A program may use at most 64 MiB of HBM per device.

v0:
```python
import math

import jax
import jax.numpy as jnp
from jax import lax
from jax.sharding import PartitionSpec as P

RADIUS = 6
PAIR_CAP = 2


MIXED_WEIGHT = 0.7
CENTER = 12.0
HALF_WIDTH = 8.0


def padded_2(shard, sides, width):
    for axis, dim in sides:
        count, length = (lax.axis_size(axis), shard.shape[dim])
        up = [(i, (i + 1) % count) for i in range(count)]
        down = [(j, i) for i, j in up]
        last = lax.slice_in_dim(shard, length - width, length, axis=dim)
        initial = lax.slice_in_dim(shard, 0, width, axis=dim)
        before = lax.ppermute(last, axis, up)
        after = lax.ppermute(initial, axis, down)
        shard = jnp.concatenate([before, shard, after], axis=dim)
    return shard


def second_table(radius):
    weights = [-2.0 * sum((1.0 / (k * k) for k in range(1, radius + 1)))]
    for k in range(1, radius + 1):
        weights.append(
            2.0
            * (-1) ** (k + 1)
            * math.factorial(radius) ** 2
            / (k * k * math.factorial(radius - k) * math.factorial(radius + k))
        )
    return weights


def first_table(radius):
    weights = [0.0]
    for k in range(1, radius + 1):
        weights.append(
            (-1) ** (k + 1)
            * math.factorial(radius) ** 2
            / (k * math.factorial(radius - k) * math.factorial(radius + k))
        )
    return weights


def laplacian(padded, plane_count):
    second_weights = second_table(RADIUS)
    first_weights = first_table(RADIUS)
    interior = padded[:, RADIUS : RADIUS + plane_count]
    line_depth = interior.shape[3]
    z_padded = jnp.pad(interior, ((0, 0), (0, 0), (0, 0), (RADIUS, RADIUS)))
    summed = 3.0 * second_weights[0] * interior
    y_slope = jnp.zeros_like(padded)
    for k in range(1, RADIUS + 1):
        summed = summed + second_weights[k] * (
            padded[:, RADIUS + k : RADIUS + k + plane_count]
            + padded[:, RADIUS - k : RADIUS - k + plane_count]
        )
        summed = summed + second_weights[k] * (jnp.roll(interior, -k, 2) + jnp.roll(interior, k, 2))
        summed = summed + second_weights[k] * (
            z_padded[:, :, :, RADIUS + k : RADIUS + k + line_depth]
            + z_padded[:, :, :, RADIUS - k : RADIUS - k + line_depth]
        )
        y_slope = y_slope + first_weights[k] * (jnp.roll(padded, -k, 2) - jnp.roll(padded, k, 2))
    cross_term = jnp.zeros_like(interior)
    for k in range(1, RADIUS + 1):
        cross_term = cross_term + first_weights[k] * (
            y_slope[:, RADIUS + k : RADIUS + k + plane_count]
            - y_slope[:, RADIUS - k : RADIUS - k + plane_count]
        )
    return summed + MIXED_WEIGHT * cross_term


def shards(states_in, potential, projectors, proj_gains, atom_owner, atom_rows, wrap_rows):
    state_count, tile_width, breadth, line_depth = states_in.shape
    n_grid = lax.axis_size("grid")
    tile_index = lax.axis_index("grid")
    tile_lines = tile_width * breadth
    block_rows = atom_rows.shape[1]
    line_span = block_rows * line_depth
    proj_count = projectors.shape[2]
    home_count = atom_owner.shape[0]
    row_order = jnp.arange(breadth, dtype=jnp.int32)
    unwrap_rows = jnp.sum(
        row_order[None, :] * (wrap_rows[None, :] == row_order[:, None]).astype(jnp.int32), axis=1
    )
    atom_order = jnp.arange(home_count, dtype=jnp.int32)
    same_owner = (atom_owner[:, None] == atom_owner[None, :]) & (
        atom_order[None, :] < atom_order[:, None]
    )
    owner_rank = jnp.sum(same_owner.astype(jnp.int32), axis=1)
    atom_slot = atom_owner * PAIR_CAP + owner_rank
    local_rows = jnp.where(atom_rows >= 0, atom_rows - tile_index * tile_lines, tile_lines)
    full_proj, full_gain = (
        lax.all_gather(projectors, "states", axis=1, tiled=True),
        lax.all_gather(proj_gains, "states", axis=1, tiled=True),
    )
    full_proj = full_proj.reshape(n_grid, PAIR_CAP, proj_count, line_span)
    full_gain = full_gain.reshape(n_grid, PAIR_CAP, proj_count)

    def extended(grid_field):
        padded = padded_2(grid_field, (("grid", 1),), RADIUS)
        low_rim = padded[:, :RADIUS]
        high_rim = padded[:, RADIUS + tile_width :]
        low_rim = jnp.where(tile_index == 0, jnp.take(low_rim, wrap_rows, axis=2), low_rim)
        high_rim = jnp.where(
            tile_index == n_grid - 1, jnp.take(high_rim, unwrap_rows, axis=2), high_rim
        )
        return jnp.concatenate([low_rim, padded[:, RADIUS : RADIUS + tile_width], high_rim], axis=1)

    def pick_rows(grid_field):
        lines_here = grid_field.reshape(state_count, tile_lines, line_depth)
        picked = jnp.take(lines_here, local_rows, axis=1, mode="fill", fill_value=0.0).astype(
            jnp.bfloat16
        )
        return jnp.swapaxes(picked.reshape(state_count, home_count, line_span), 0, 1)

    def place_rows(projected):
        pieces = (
            jnp.swapaxes(projected, 0, 1)
            .reshape(state_count, home_count, block_rows, line_depth)
            .astype(jnp.float32)
        )
        summed = (
            jnp.zeros((state_count, tile_lines, line_depth), jnp.float32)
            .at[:, local_rows]
            .add(pieces, mode="drop")
        )
        return summed.reshape(state_count, tile_width, breadth, line_depth)

    def at_owner(received):
        coefficients = jnp.einsum(
            "gpjc,gpsc->gpsj", full_proj, received, preferred_element_type=jnp.float32
        )
        scaled = (coefficients * full_gain[:, :, None, :].astype(jnp.float32)).astype(jnp.bfloat16)
        projected = jnp.einsum(
            "gpjc,gpsj->gpsc", full_proj, scaled, preferred_element_type=jnp.float32
        ).astype(jnp.bfloat16)
        return lax.all_to_all(projected, "grid", split_axis=0, concat_axis=0, tiled=True)

    def nonlocal_part(grid_field):
        picked = pick_rows(grid_field)
        outbox = (
            jnp.zeros((n_grid * PAIR_CAP, state_count, line_span), jnp.bfloat16)
            .at[atom_slot]
            .set(picked)
        )
        outbox = outbox.reshape(n_grid, PAIR_CAP, state_count, line_span)
        returned_rows = at_owner(
            lax.all_to_all(outbox, "grid", split_axis=0, concat_axis=0, tiled=True)
        )
        projected = jnp.take(
            returned_rows.reshape(n_grid * PAIR_CAP, state_count, line_span), atom_slot, axis=0
        )
        return place_rows(projected)

    def operate(grid_field):
        padded = extended(grid_field)
        return (
            -0.5 * laplacian(padded, tile_width)
            + potential[None] * grid_field
            + nonlocal_part(grid_field)
        )

    def shifted(grid_field):
        return (operate(grid_field) - CENTER * grid_field) / HALF_WIDTH

    first_term = shifted(states_in)
    second_term = 2.0 * shifted(first_term) - states_in
    return 2.0 * shifted(second_term) - first_term


def solution(mesh):
    in_specs = (
        P("states", "grid", None, None),
        P("grid", None, None),
        P("grid", "states", None, None),
        P("grid", "states", None),
        P("grid"),
        P("grid", None),
        P(),
    )
    out_specs = P("states", "grid", None, None)
    return jax.shard_map(shards, mesh=mesh, in_specs=in_specs, out_specs=out_specs, check_vma=False)
```

profile of v0, /device:TPU:0, one launch (start us, length us, event | category | flops | bytes accessed | tf_op | source)
XLA Modules:
  0.0 187.1 jit_solution(12501235781141206457)
XLA Ops:
  7.7 6.1 %collective-permute-start = (f32[1,6,32,128]{3,1,2,0:T(8,128)S(1)}, f32[1,6,32,128]{3,1,2,0:T(8,128)S(1)}, u32[]{:S(2)}, u32[]{:S(2)}) collective-permute-start(f32[1,6,32,128]{3,1,2,0:T(8,128)S(1)} %get-tuple-element.157), channel_id=1, source_target_pairs={{4,0},{8,4},{12,8},{16,12},{20,16},{24,20},{28,24},{0,28},{5,1},{9... | collective-permute-start | bytes 294920 | tf_op jit(solution)/shard_map/ppermute | solution.py:25
  18.1 6.0 %all-to-all-start = ((bf16[8,2,1,4096]{3,1,2,0:T(2,128)(2,1)}), bf16[8,2,1,4096]{3,1,2,0:T(2,128)(2,1)S(1)}, u32[]{:S(2)}, u32[]{:S(2)}) async-start(bf16[8,2,1,4096]{3,1,2,0:T(2,128)(2,1)} %reshape.2251), calls=%async_computation | async-start | bytes 262144 | tf_op jit(solution)/shard_map/all_to_all | solution.py:157
  33.8 5.2 %all_gather.7 = bf16[1,16,8]{2,0,1:T(2,128)(2,1)S(1)} all-gather(bf16[1,4,8]{2,0,1:T(2,128)(2,1)S(1)} %copy.163), channel_id=1, replica_groups=mesh['grid'=8,'states'=4] {'states'}, dimensions={1}, use_global_device_ids=true | all-gather | bytes 320 | tf_op jit(solution)/shard_map/all_gather | solution.py:103
  47.0 2.1 %fusion.275 = f32[8,2,1,8]{3,2,1,0:T(1,128)S(1)} fusion(bf16[8,2,8,4096]{3,2,1,0:T(8,128)(2,1)} %bitcast.159, bf16[8,2,4096,1]{2,1,0,3:T(2,128)(2,1)S(1)} %bitcast.184), kind=kOutput, calls=%fused_computation.467 | convolution fusion | flops 1048576 | bytes 1180160 | tf_op jit(solution)/shard_map/gpjc,gpsc->gpsj/dot_general | solution.py:139
  50.5 6.0 %all-to-all-start.1 = ((bf16[8,2,1,4096]{3,1,2,0:T(2,128)(2,1)}), bf16[8,2,1,4096]{3,1,2,0:T(2,128)(2,1)S(1)}, u32[]{:S(2)}, u32[]{:S(2)}) async-start(bf16[8,2,1,4096]{3,1,2,0:T(2,128)(2,1)} %bitcast.154), calls=%async_computation.1 | async-start | bytes 262144 | tf_op jit(solution)/shard_map/all_to_all | solution.py:146
  56.4 3.3 %fusion.25 = f32[1,28,32,128]{3,1,2,0:T(8,128)S(1)} fusion(f32[1,6,32,128]{3,1,2,0:T(8,128)S(1)} %fusion.285, f32[1,16,32,128]{3,1,2,0:T(8,128)S(1)} %copy.129, f32[1,6,32,128]{3,1,2,0:T(8,128)S(1)} %fusion.284, f32[1,28,31,128]{3,1,2,0:T(8,128)} %get-tuple-element.79, f32[1,28,31,128]{3,1,2,0:T(8,128)} %get-tuple-element.78, ...), kind=kLoop, calls=%fused_computation.148 | loop fusion | flops 3784704 | bytes 6393856 | tf_op jit(solution)/shard_map/add | solution.py:71
  59.8 4.1 %all-to-all-done.1 = bf16[8,2,1,4096]{3,1,2,0:T(2,128)(2,1)S(1)} async-done(((bf16[8,2,1,4096]{3,1,2,0:T(2,128)(2,1)}), bf16[8,2,1,4096]{3,1,2,0:T(2,128)(2,1)S(1)}, u32[]{:S(2)}, u32[]{:S(2)}) %all-to-all-start.1) | async-done | bytes 131104 | tf_op jit(solution)/shard_map/all_to_all | solution.py:146
  64.7 2.0 %scatter_custom_fusion.1 = f32[512,128]{1,0:T(8,128)S(1)} fusion(s32[320]{0:T(512)} %copy-done.27, f32[320,128]{1,0:T(8,128)S(1)} %reshape.2406, f32[]{:T(128)} %constant.24.clone.1), kind=kCustom, calls=%fused_computation.497 | custom fusion | flops 40960 | bytes 262656 | tf_op jit(solution)/shard_map/scatter-add | solution.py:134
  67.5 3.5 %broadcast_multiply_fusion = (f32[1,16,32,128]{3,1,2,0:T(8,128)S(1)}, f32[1,16,32,128]{3,1,2,0:T(8,128)S(1)}) fusion(f32[1,16,32,128]{3,1,2,0:T(8,128)S(1)} %copy.129, f32[1,16,32,128]{3,2,1,0:T(8,128)S(1)} %bitcast.169, f32[16,32,128]{2,1,0:T(8,128)S(1)} %copy-done.2, f32[1,28,32,128]{3,1,2,0:T(8,128)S(1)} %fusion.25, ...), kind=kLoop, calls=%fused_computation.499 | loop fusion | flops 6881280 | bytes 7798784 | tf_op jit(solution)/shard_map/div | solution.py:173
  85.1 5.4 %all-to-all-start.2 = ((bf16[8,2,1,4096]{3,1,2,0:T(2,128)(2,1)}), bf16[8,2,1,4096]{3,1,2,0:T(2,128)(2,1)}, u32[]{:S(2)}, u32[]{:S(2)}) async-start(bf16[8,2,1,4096]{3,1,2,0:T(2,128)(2,1)} %reshape.2257), calls=%async_computation.2 | async-start | bytes 262144 | tf_op jit(solution)/shard_map/all_to_all | solution.py:157
  100.5 1.7 fusion.273
  103.5 6.0 %all-to-all-start.3 = ((bf16[8,2,1,4096]{3,1,2,0:T(2,128)(2,1)}), bf16[8,2,1,4096]{3,1,2,0:T(2,128)(2,1)S(1)}, u32[]{:S(2)}, u32[]{:S(2)}) async-start(bf16[8,2,1,4096]{3,1,2,0:T(2,128)(2,1)} %bitcast.156), calls=%async_computation.3 | async-start | bytes 262144 | tf_op jit(solution)/shard_map/all_to_all | solution.py:146
  110.3 3.4 %fusion.16 = f32[1,28,32,128]{3,1,2,0:T(8,128)S(1)} fusion(f32[1,6,32,128]{3,1,2,0:T(8,128)S(1)} %fusion.283, f32[1,16,32,128]{3,1,2,0:T(8,128)S(1)} %get-tuple-element.6, f32[1,6,32,128]{3,1,2,0:T(8,128)S(1)} %fusion.282, f32[1,28,31,128]{3,1,2,0:T(8,128)} %get-tuple-element.57, f32[1,28,31,128]{3,1,2,0:T(8,128)} %get-tuple-element.56, ...), kind=kLoop, calls=%fused_computation.135 | loop fusion | flops 3784704 | bytes 6393856 | tf_op jit(solution)/shard_map/add | solution.py:71
  113.7 3.1 %all-to-all-done.3 = bf16[8,2,1,4096]{3,1,2,0:T(2,128)(2,1)S(1)} async-done(((bf16[8,2,1,4096]{3,1,2,0:T(2,128)(2,1)}), bf16[8,2,1,4096]{3,1,2,0:T(2,128)(2,1)S(1)}, u32[]{:S(2)}, u32[]{:S(2)}) %all-to-all-start.3) | async-done | bytes 131104 | tf_op jit(solution)/shard_map/all_to_all | solution.py:146
  118.4 2.1 %scatter_custom_fusion.3 = f32[512,128]{1,0:T(8,128)S(1)} fusion(s32[320]{0:T(512)} %copy-done.27, f32[320,128]{1,0:T(8,128)} %reshape.2426, f32[]{:T(128)} %constant.24.clone.1), kind=kCustom, calls=%fused_computation.495 | custom fusion | flops 40960 | bytes 262656 | tf_op jit(solution)/shard_map/scatter-add | solution.py:134
  121.3 3.7 %fusion.102 = f32[1,16,32,128]{3,1,2,0:T(8,128)S(1)} fusion(f32[1,16,32,128]{3,1,2,0:T(8,128)S(1)} %get-tuple-element.6, f32[1,6,32,128]{3,1,2,0:T(8,128)S(1)} %fusion.282, f32[1,6,32,128]{3,1,2,0:T(8,128)S(1)} %fusion.283, f32[1,28,32,128]{3,1,2,0:T(8,128)S(1)} %fusion.16, f32[1,16,1,128]{3,1,2,0:T(8,128)} %get-tuple-element.127, ...), kind=kLoop, calls=%fused_computation.246 | loop fusion | flops 6946816 | bytes 8060928 | tf_op jit(solution)/shard_map/sub | solution.py:176
  133.3 1.6 collective-permute-start.4
  139.1 5.6 %all-to-all-start.4 = ((bf16[8,2,1,4096]{3,1,2,0:T(2,128)(2,1)}), bf16[8,2,1,4096]{3,1,2,0:T(2,128)(2,1)}, u32[]{:S(2)}, u32[]{:S(2)}) async-start(bf16[8,2,1,4096]{3,1,2,0:T(2,128)(2,1)} %reshape.2262), calls=%async_computation.4 | async-start | bytes 262144 | tf_op jit(solution)/shard_map/all_to_all | solution.py:157
  155.9 1.7 fusion.271
  158.9 6.0 %all-to-all-start.5 = ((bf16[8,2,1,4096]{3,1,2,0:T(2,128)(2,1)}), bf16[8,2,1,4096]{3,1,2,0:T(2,128)(2,1)S(1)}, u32[]{:S(2)}, u32[]{:S(2)}) async-start(bf16[8,2,1,4096]{3,1,2,0:T(2,128)(2,1)} %bitcast.158), calls=%async_computation.5 | async-start | bytes 262144 | tf_op jit(solution)/shard_map/all_to_all | solution.py:146
  165.8 3.1 %fusion.7 = f32[1,28,32,128]{3,1,2,0:T(8,128)S(1)} fusion(f32[1,6,32,128]{3,1,2,0:T(8,128)S(1)} %fusion.281, f32[1,16,32,128]{3,1,2,0:T(8,128)S(1)} %fusion.102, f32[1,6,32,128]{3,1,2,0:T(8,128)S(1)} %fusion.280, f32[1,28,31,128]{3,1,2,0:T(8,128)S(1)} %copy-done.3, f32[1,28,31,128]{3,1,2,0:T(8,128)S(1)} %get-tuple-element.34, ...), kind=kLoop, calls=%fused_computation.122 | loop fusion | flops 3784704 | bytes 6393856 | tf_op jit(solution)/shard_map/add | solution.py:71
  168.9 3.3 %all-to-all-done.5 = bf16[8,2,1,4096]{3,1,2,0:T(2,128)(2,1)S(1)} async-done(((bf16[8,2,1,4096]{3,1,2,0:T(2,128)(2,1)}), bf16[8,2,1,4096]{3,1,2,0:T(2,128)(2,1)S(1)}, u32[]{:S(2)}, u32[]{:S(2)}) %all-to-all-start.5) | async-done | bytes 131104 | tf_op jit(solution)/shard_map/all_to_all | solution.py:146
  173.4 2.0 %scatter_custom_fusion.5 = f32[512,128]{1,0:T(8,128)S(1)} fusion(s32[320]{0:T(512)} %copy-done.27, f32[320,128]{1,0:T(8,128)S(1)} %reshape.2446, f32[]{:T(128)} %constant.24.clone.1), kind=kCustom, calls=%fused_computation.493 | custom fusion | flops 40960 | bytes 262656 | tf_op jit(solution)/shard_map/scatter-add | solution.py:134
  176.1 3.3 %fusion.57 = f32[1,16,32,128]{3,1,2,0:T(8,128)S(1)} fusion(f32[1,16,32,128]{3,1,2,0:T(8,128)S(1)} %fusion.102, f32[1,6,32,128]{3,1,2,0:T(8,128)S(1)} %fusion.280, f32[1,6,32,128]{3,1,2,0:T(8,128)S(1)} %fusion.281, f32[1,28,32,128]{3,1,2,0:T(8,128)S(1)} %fusion.7, f32[1,16,1,128]{3,1,2,0:T(8,128)} %get-tuple-element.101, ...), kind=kLoop, calls=%fused_computation.201 | loop fusion | flops 7012352 | bytes 7798784 | tf_op jit(solution)/shard_map/sub | solution.py:177
  (245 shorter events, 82.4 us)
Async XLA Ops:
  7.6 6.8 %copy-start.1 = (f32[1,16,32,128]{3,2,1,0:T(8,128)S(1)}, f32[1,16,32,128]{3,2,1,0:T(8,128)}, u32[]{:S(2)}) copy-start(f32[1,16,32,128]{3,2,1,0:T(8,128)} %param.13) | copy-start | bytes 786436
  7.7 6.1 %copy-start.28 = (s32[10,32]{1,0:T(8,128)S(1)}, s32[10,32]{1,0:T(8,128)}, u32[]{:S(2)}) copy-start(s32[10,32]{1,0:T(8,128)} %param.18) | copy-start | bytes 3844
  7.7 31.3 %collective-permute-start = (f32[1,6,32,128]{3,1,2,0:T(8,128)S(1)}, f32[1,6,32,128]{3,1,2,0:T(8,128)S(1)}, u32[]{:S(2)}, u32[]{:S(2)}) collective-permute-start(f32[1,6,32,128]{3,1,2,0:T(8,128)S(1)} %get-tuple-element.157), channel_id=1, source_target_pairs={{4,0},{8,4},{12,8},{16,12},{20,16},{24,20},{28,24},{0,28},{5,1},{9... | collective-permute-start | bytes 294920 | tf_op jit(solution)/shard_map/ppermute | solution.py:25
  13.8 25.9 %collective-permute-start.1 = (f32[1,6,32,128]{3,1,2,0:T(8,128)S(1)}, f32[1,6,32,128]{3,1,2,0:T(8,128)S(1)}, u32[]{:S(2)}, u32[]{:S(2)}) collective-permute-start(f32[1,6,32,128]{3,1,2,0:T(8,128)S(1)} %get-tuple-element.156), channel_id=1, source_target_pairs={{0,4},{4,8},{8,12},{12,16},{16,20},{20,24},{24,28},{28,0},{1,5},{5... | collective-permute-start | bytes 294920 | tf_op jit(solution)/shard_map/ppermute | solution.py:24
  16.6 8.5 %copy-start.38 = (s32[10]{0:T(128)}, s32[10]{0:T(128)S(1)}, u32[]{:S(2)}) copy-start(s32[10]{0:T(128)S(1)} %get-tuple-element.11) | copy-start | bytes 124
  16.6 48.0 %copy-start.24 = (pred[10]{0:T(512)(128)(4,1)}, pred[10]{0:T(512)(128)(4,1)S(1)}, u32[]{:S(2)}) copy-start(pred[10]{0:T(512)(128)(4,1)S(1)} %get-tuple-element.10) | copy-start | bytes 34
  18.1 28.9 %all-to-all-start = ((bf16[8,2,1,4096]{3,1,2,0:T(2,128)(2,1)}), bf16[8,2,1,4096]{3,1,2,0:T(2,128)(2,1)S(1)}, u32[]{:S(2)}, u32[]{:S(2)}) async-start(bf16[8,2,1,4096]{3,1,2,0:T(2,128)(2,1)} %reshape.2251), calls=%async_computation | async-start | bytes 262144 | tf_op jit(solution)/shard_map/all_to_all | solution.py:157
  24.1 22.9 %all-gather.2.cloned.1.call-start = ((), (), s32[]{:S(2)}) async-start(), calls=%async_computation.6 | async-start | bytes 1310720 | tf_op jit(solution)/shard_map/all_gather | solution.py:102
  25.0 15.3 %copy-start.35 = (pred[32]{0:T(512)(128)(4,1)}, pred[32]{0:T(512)(128)(4,1)S(1)}, u32[]{:S(2)}) copy-start(pred[32]{0:T(512)(128)(4,1)S(1)} %compare_and_fusion.3) | copy-start | bytes 100
  25.0 15.3 %copy-start.32 = (pred[32]{0:T(512)(128)(4,1)}, pred[32]{0:T(512)(128)(4,1)S(1)}, u32[]{:S(2)}) copy-start(pred[32]{0:T(512)(128)(4,1)S(1)} %compare_and_fusion.2) | copy-start | bytes 100
  25.0 38.9 %copy-start.29 = (s32[1024]{0:T(1024)}, s32[1024]{0:T(1024)S(1)}, u32[]{:S(2)}) copy-start(s32[1024]{0:T(1024)S(1)} %pad_clamp_fusion) | copy-start | bytes 12292
  33.1 5.9 %copy-start.30 = (s32[1024]{0:T(1024)}, s32[1024]{0:T(1024)S(1)}, u32[]{:S(2)}) copy-start(s32[1024]{0:T(1024)S(1)} %pad_clamp_fusion.3) | copy-start | bytes 12292
  39.0 63.2 %copy-start.18 = (bf16[1,16,8]{2,1,0:T(8,128)(2,1)}, bf16[1,16,8]{2,1,0:T(8,128)(2,1)S(1)}, u32[]{:S(2)}) copy-start(bf16[1,16,8]{2,1,0:T(8,128)(2,1)S(1)} %copy.164) | copy-start | bytes 772
  50.5 13.4 %all-to-all-start.1 = ((bf16[8,2,1,4096]{3,1,2,0:T(2,128)(2,1)}), bf16[8,2,1,4096]{3,1,2,0:T(2,128)(2,1)S(1)}, u32[]{:S(2)}, u32[]{:S(2)}) async-start(bf16[8,2,1,4096]{3,1,2,0:T(2,128)(2,1)} %bitcast.154), calls=%async_computation.1 | async-start | bytes 262144 | tf_op jit(solution)/shard_map/all_to_all | solution.py:146
  79.1 11.3 %collective-permute-start.2 = (f32[1,6,32,128]{3,1,2,0:T(8,128)S(1)}, f32[1,6,32,128]{3,1,2,0:T(8,128)S(1)}, u32[]{:S(2)}, u32[]{:S(2)}) collective-permute-start(f32[1,6,32,128]{3,1,2,0:T(8,128)S(1)} %get-tuple-element.130), channel_id=1, source_target_pairs={{4,0},{8,4},{12,8},{16,12},{20,16},{24,20},{28,24},{0,28},{5,1},{9... | collective-permute-start | bytes 294920 | tf_op jit(solution)/shard_map/ppermute | solution.py:25
  80.6 10.6 %collective-permute-start.3 = (f32[1,6,32,128]{3,1,2,0:T(8,128)S(1)}, f32[1,6,32,128]{3,1,2,0:T(8,128)S(1)}, u32[]{:S(2)}, u32[]{:S(2)}) collective-permute-start(f32[1,6,32,128]{3,1,2,0:T(8,128)S(1)} %get-tuple-element.131), channel_id=1, source_target_pairs={{0,4},{4,8},{8,12},{12,16},{16,20},{20,24},{24,28},{28,0},{1,5},{5... | collective-permute-start | bytes 294920 | tf_op jit(solution)/shard_map/ppermute | solution.py:24
  85.1 15.4 %all-to-all-start.2 = ((bf16[8,2,1,4096]{3,1,2,0:T(2,128)(2,1)}), bf16[8,2,1,4096]{3,1,2,0:T(2,128)(2,1)}, u32[]{:S(2)}, u32[]{:S(2)}) async-start(bf16[8,2,1,4096]{3,1,2,0:T(2,128)(2,1)} %reshape.2257), calls=%async_computation.2 | async-start | bytes 262144 | tf_op jit(solution)/shard_map/all_to_all | solution.py:157
  103.5 13.3 %all-to-all-start.3 = ((bf16[8,2,1,4096]{3,1,2,0:T(2,128)(2,1)}), bf16[8,2,1,4096]{3,1,2,0:T(2,128)(2,1)S(1)}, u32[]{:S(2)}, u32[]{:S(2)}) async-start(bf16[8,2,1,4096]{3,1,2,0:T(2,128)(2,1)} %bitcast.156), calls=%async_computation.3 | async-start | bytes 262144 | tf_op jit(solution)/shard_map/all_to_all | solution.py:146
  131.4 5.3 %copy-start.22 = (pred[10,32]{1,0:T(8,128)(4,1)S(1)}, pred[10,32]{1,0:T(8,128)(4,1)}, u32[]{:S(2)}) copy-start(pred[10,32]{1,0:T(8,128)(4,1)} %copy-done.20) | copy-start | bytes 964
  133.3 11.5 %collective-permute-start.4 = (f32[1,6,32,128]{3,1,2,0:T(8,128)S(1)}, f32[1,6,32,128]{3,1,2,0:T(8,128)S(1)}, u32[]{:S(2)}, u32[]{:S(2)}) collective-permute-start(f32[1,6,32,128]{3,1,2,0:T(8,128)S(1)} %get-tuple-element.104), channel_id=1, source_target_pairs={{4,0},{8,4},{12,8},{16,12},{20,16},{24,20},{28,24},{0,28},{5,1},{9... | collective-permute-start | bytes 294920 | tf_op jit(solution)/shard_map/ppermute | solution.py:25
  134.9 10.6 %collective-permute-start.5 = (f32[1,6,32,128]{3,1,2,0:T(8,128)S(1)}, f32[1,6,32,128]{3,1,2,0:T(8,128)S(1)}, u32[]{:S(2)}, u32[]{:S(2)}) collective-permute-start(f32[1,6,32,128]{3,1,2,0:T(8,128)S(1)} %get-tuple-element.105), channel_id=1, source_target_pairs={{0,4},{4,8},{8,12},{12,16},{16,20},{20,24},{24,28},{28,0},{1,5},{5... | collective-permute-start | bytes 294920 | tf_op jit(solution)/shard_map/ppermute | solution.py:24
  139.1 16.8 %all-to-all-start.4 = ((bf16[8,2,1,4096]{3,1,2,0:T(2,128)(2,1)}), bf16[8,2,1,4096]{3,1,2,0:T(2,128)(2,1)}, u32[]{:S(2)}, u32[]{:S(2)}) async-start(bf16[8,2,1,4096]{3,1,2,0:T(2,128)(2,1)} %reshape.2262), calls=%async_computation.4 | async-start | bytes 262144 | tf_op jit(solution)/shard_map/all_to_all | solution.py:157
  158.0 6.9 %copy-start.3 = (f32[1,28,31,128]{3,1,2,0:T(8,128)S(1)}, f32[1,28,31,128]{3,1,2,0:T(8,128)}, u32[]{:S(2)}) copy-start(f32[1,28,31,128]{3,1,2,0:T(8,128)} %get-tuple-element.35) | copy-start | bytes 1333252
  158.9 13.3 %all-to-all-start.5 = ((bf16[8,2,1,4096]{3,1,2,0:T(2,128)(2,1)}), bf16[8,2,1,4096]{3,1,2,0:T(2,128)(2,1)S(1)}, u32[]{:S(2)}, u32[]{:S(2)}) async-start(bf16[8,2,1,4096]{3,1,2,0:T(2,128)(2,1)} %bitcast.158), calls=%async_computation.5 | async-start | bytes 262144 | tf_op jit(solution)/shard_map/all_to_all | solution.py:146
  (31 other events, 41.4 us)
Sparse Core Ops, SparseCore 0:
  26.5 18.1 all-gather.1
where the time goes:
time: 188 us; the launch traced here: 187 us
  local copies, waits for them, and re-layouts  76.2 us (41%)
  starting transfers between devices  45.1 us (24%)
  other arithmetic  28.2 us (15%)
  between operations  14.5 us (8%)
  waiting for transfers between devices  11.2 us (6%)
  matrix products  6.7 us (4%)
  blocking collectives  5.16 us (3%)
    slice x33, local copies, waits for them, and re-layouts, laplacian(): jnp.roll(padded, k, 2)  22.9 us
    all_to_all x3, starting transfers between devices, at_owner(): lax.all_to_all(projected, 'grid', split_axis=0, concat_axis=0, tiled=True)  18 us
    slice x24, local copies, waits for them, and re-layouts, laplacian(): jnp.roll(interior, k, 2)  17.4 us
    all_to_all x3, starting transfers between devices, nonlocal_part(): lax.all_to_all(outbox, 'grid', split_axis=0, concat_axis=0, tiled=True)  17 us
    all_to_all x3, waiting for transfers between devices, at_owner(): lax.all_to_all(projected, 'grid', split_axis=0, concat_axis=0, tiled=True)  10.5 us
    add x3, other arithmetic, laplacian(): y_slope + first_weights[k] * (jnp.roll(padded, -k, 2) - jnp.roll(padded,...  9.85 us
    ppermute x3, starting transfers between devices, padded_2(): after = lax.ppermute(initial, axis, down)  9.14 us
    unnamed x92, local copies, waits for them, and re-layouts  8.3 us
  transfers between devices with their start and end apart: 13, of which 3 were waited for; matrix products, arithmetic and copies ran while one was open for 30% of the time, Pallas kernels for 0%

commit v1 on v0

v1 whole, which is shorter than its diff:
```python
import functools
import math

import jax
import jax.numpy as jnp
import ml_dtypes
import numpy as np
from jax import lax
from jax.experimental import pallas as pl
from jax.experimental.pallas import tpu as pltpu
from jax.sharding import PartitionSpec as P

RADIUS = 6
PAIR_CAP = 2
ATOM_PAD = 16

MIXED_WEIGHT = 0.7
CENTER = 12.0
HALF_WIDTH = 8.0

MESH = pl.DeviceIdType.MESH
F32 = jnp.float32
BF16 = jnp.bfloat16


def second_table(radius):
    weights = [-2.0 * sum((1.0 / (k * k) for k in range(1, radius + 1)))]
    for k in range(1, radius + 1):
        weights.append(
            2.0
            * (-1) ** (k + 1)
            * math.factorial(radius) ** 2
            / (k * k * math.factorial(radius - k) * math.factorial(radius + k))
        )
    return weights


def first_table(radius):
    weights = [0.0]
    for k in range(1, radius + 1):
        weights.append(
            (-1) ** (k + 1)
            * math.factorial(radius) ** 2
            / (k * math.factorial(radius - k) * math.factorial(radius + k))
        )
    return weights


def stencil_matrices(planes, breadth, depth):
    second, first = second_table(RADIUS), first_table(RADIUS)
    factor = -0.5 / HALF_WIDTH
    steps = range(1, RADIUS + 1)
    wide = planes + 2 * RADIUS
    lines = np.zeros((planes, breadth, wide, breadth))
    rows = np.arange(breadth)
    for x in range(planes):
        centre = x + RADIUS
        for k in steps:
            for sign in (1, -1):
                lines[x, rows, centre + sign * k, rows] += second[k]
                lines[x, rows, centre, (rows + sign * k) % breadth] += second[k]
                for j in steps:
                    for turn in (1, -1):
                        lines[x, rows, centre + sign * k, (rows + turn * j) % breadth] += (
                            MIXED_WEIGHT * sign * turn * first[k] * first[j]
                        )
    lines = factor * lines.reshape(planes * breadth, wide * breadth)
    across = np.zeros((depth, depth))
    for k in steps:
        across += second[k] * (np.eye(depth, k=k) + np.eye(depth, k=-k))
    rim = RADIUS * breadth
    inner = lines[:, rim:-rim]
    low = lines[:rim, :rim]
    high = lines[-rim:, -rim:]
    return inner, low, high, factor * across, factor * 3.0 * second[0]


def halves(matrix):
    high = matrix.astype(ml_dtypes.bfloat16)
    low = (matrix - high.astype(np.float64)).astype(ml_dtypes.bfloat16)
    return high, low


def dot(a, b):
    return jnp.dot(a, b, preferred_element_type=F32)


def kernel(
    dims,
    v_ref,
    pot_ref,
    proj_ref,
    gain_ref,
    owner_ref,
    rows_ref,
    wrap_ref,
    inner_h_ref,
    inner_l_ref,
    rim_ref,
    across_ref,
    out_ref,
    sendbuf,
    arrived,
    parts,
    hi_ref,
    halo,
    pick_ref,
    place_ref,
    rim_turned,
    base_ref,
    part_send,
    part_recv,
    share_send,
    share_recv,
    halo_send,
    halo_recv,
):
    n_grid, n_states, tiles, chunk, breadth, nproj, atoms, centre_weight = dims
    cells, depth = v_ref.shape
    rim = RADIUS * breadth
    blocks = chunk // depth
    slot_rows = PAIR_CAP * nproj
    me_g, me_s = lax.axis_index("grid"), lax.axis_index("states")
    up, down = lax.rem(me_g + 1, n_grid), lax.rem(me_g + n_grid - 1, n_grid)
    holder = me_g // tiles
    partner = me_s + 1 - 2 * lax.rem(me_s, 2)
    twins = [lax.rem(me_s + 2 * d, n_states) for d in range(1, n_states // 2)]

    barrier = pltpu.get_barrier_semaphore()

    def greet(g, s):
        pl.semaphore_signal(barrier, inc=1, device_id=(g, s), device_id_type=MESH)

    for o in range(n_grid):

        @pl.when((me_g != o) | (holder != me_s))
        def _():
            greet(o, holder)

    greet(up, me_s)
    greet(down, me_s)
    greet(me_g, partner)
    for s in twins:
        greet(me_g, s)

    for i in range(tiles):
        held = pl.ds(i * slot_rows, slot_rows)
        for s in range(n_states):
            sendbuf[i, s, :, :chunk] = proj_ref[held, s * chunk : (s + 1) * chunk]
            sendbuf[i, s, :, chunk:] = gain_ref[held, :]
    hi_ref[0] = v_ref[...].astype(BF16)

    pl.semaphore_wait(barrier, n_grid + 2 + len(twins) + jnp.where(holder == me_s, 0, 1))

    def part_copy(i, d):
        s = lax.rem(me_s + d, n_states)
        return pltpu.make_async_remote_copy(
            src_ref=sendbuf.at[i, s],
            dst_ref=arrived.at[me_g],
            send_sem=part_send.at[i, d],
            recv_sem=part_recv.at[me_g],
            device_id=(me_s * tiles + i, s),
            device_id_type=MESH,
        )

    def halo_copies(step):
        return [
            pltpu.make_async_remote_copy(
                src_ref=hi_ref.at[step, pl.ds(start, rim)],
                dst_ref=halo.at[step, side],
                send_sem=halo_send.at[step, side],
                recv_sem=halo_recv.at[step, side],
                device_id=(target, me_s),
                device_id_type=MESH,
            )
            for side, start, target in ((0, cells - rim, up), (1, 0, down))
        ]

    def share_copy(index, part, target):
        return pltpu.make_async_remote_copy(
            src_ref=parts.at[part],
            dst_ref=parts.at[part],
            send_sem=share_send.at[index],
            recv_sem=share_recv.at[part],
            device_id=(me_g, target),
            device_id_type=MESH,
        )

    for d in range(n_states - 1, -1, -1):
        for i in range(tiles):
            if d:
                part_copy(i, d).start()
            else:

                @pl.when(me_s * tiles + i != me_g)
                def _():
                    part_copy(i, 0).start()

                @pl.when(me_s * tiles + i == me_g)
                def _():
                    arrived[me_g] = sendbuf[i, me_s]

    for copy in halo_copies(0):
        copy.start()

    owners = [owner_ref[a] for a in range(atoms)]
    slots = []
    for a in range(atoms):
        rank = jnp.int32(0)
        for b in range(a):
            rank = rank + jnp.where(owners[b] == owners[a], 1, 0)
        slots.append(owners[a] * PAIR_CAP + rank)
    width = n_grid * slot_rows
    lane = lax.broadcasted_iota(jnp.int32, (nproj, width), 1)
    row = lax.broadcasted_iota(jnp.int32, (nproj, width), 0)
    chosen = jnp.concatenate(
        [jnp.where(lane == slots[a] * nproj + row, 1.0, 0.0) for a in range(atoms)], axis=0
    ).astype(BF16)

    block_rows = rows_ref.shape[1]
    local = rows_ref[...] - me_g * cells
    local = jnp.concatenate(
        [local, jnp.full((ATOM_PAD - atoms, block_rows), -1, jnp.int32)], axis=0
    )
    line = lax.broadcasted_iota(jnp.int32, (ATOM_PAD, cells), 1)
    pick = jnp.concatenate(
        [jnp.where(local[:, b : b + 1] == line, 1.0, 0.0) for b in range(block_rows)], axis=0
    )
    pick_ref[...] = pick.astype(BF16)
    place_ref[...] = pick.T.astype(BF16)

    turn = wrap_ref[0]
    source = lax.broadcasted_iota(jnp.int32, (rim, rim), 0)
    target = lax.broadcasted_iota(jnp.int32, (rim, rim), 1)
    low_turn = jnp.where(me_g == 0, turn, 0)
    high_turn = jnp.where(me_g == n_grid - 1, breadth - turn, 0)
    for side, shift in ((0, low_turn), (1, high_turn)):
        same_plane = (source // breadth) == (target // breadth)
        moved = lax.rem(lax.rem(source, breadth) + shift, breadth) == lax.rem(target, breadth)
        permute = jnp.where(same_plane & moved, 1.0, 0.0).astype(BF16)
        for half in range(2):
            rim_turned[side, half] = dot(rim_ref[side, half], permute).astype(BF16)

    base_ref[...] = (pot_ref[...] - CENTER) * (1.0 / HALF_WIDTH) + centre_weight

    def own_cells(step, field):
        hi = hi_ref[step]
        lo = (field - hi.astype(F32)).astype(BF16)
        both = jnp.concatenate([hi, lo], axis=1)
        wide = dot(inner_h_ref[...], both)
        total = base_ref[...] * field
        total = total + (wide[:, :depth] + wide[:, depth:] + dot(inner_l_ref[...], hi))
        across = dot(hi, across_ref[...])
        total = total + (across[:, :depth] + across[:, depth:])
        return total + dot(lo, across_ref[:, :depth])

    def rims(step):
        for copy in halo_copies(step):
            copy.wait_recv()
        sums = []
        for side in range(2):
            came = halo[step, side]
            sums.append(dot(rim_turned[side, 0], came) + dot(rim_turned[side, 1], came))
        middle = jnp.zeros((cells - 2 * rim, depth), F32)
        return jnp.concatenate([sums[0], middle, sums[1]], axis=0)

    def nonlocal_part(step, gains):
        picked = dot(pick_ref[...], hi_ref[step]).astype(BF16)
        coefficients = jnp.zeros((ATOM_PAD, atoms * nproj), F32)
        for q in range(n_states):
            lines = [
                picked[(q * blocks + b) * ATOM_PAD : (q * blocks + b + 1) * ATOM_PAD]
                for b in range(blocks)
            ]
            coefficients = coefficients + lax.dot_general(
                jnp.concatenate(lines, axis=1),
                parts[q],
                (((1,), (1,)), ((), ())),
                preferred_element_type=F32,
            )
        atom = lax.broadcasted_iota(jnp.int32, coefficients.shape, 0)
        column = lax.broadcasted_iota(jnp.int32, coefficients.shape, 1)
        scaled = jnp.where(column // nproj == atom, coefficients * gains, 0.0).astype(BF16)
        pieces = []
        for q in range(n_states):
            projected = dot(scaled, parts[q]).astype(BF16)
            pieces += [projected[:, b * depth : (b + 1) * depth] for b in range(blocks)]
        return dot(place_ref[...], jnp.concatenate(pieces, axis=0)) * (1.0 / HALF_WIDTH)

    start = v_ref[...]
    first = own_cells(0, start)
    first = first + rims(0)

    for o in range(n_grid):

        @pl.when((me_g != o) | (holder != me_s))
        def _():
            pltpu.make_async_remote_copy(
                src_ref=sendbuf.at[0, 0],
                dst_ref=arrived.at[o],
                send_sem=part_send.at[0, 0],
                recv_sem=part_recv.at[o],
                device_id=(o, holder),
                device_id_type=MESH,
            ).wait_recv()

    mine = dot(chosen, arrived[...].reshape(width, chunk + depth))
    parts[me_s] = mine[:, :chunk].astype(BF16)
    for index, s in enumerate(twins):
        share_copy(1 + index, me_s, s).start()
    share_copy(0, me_s, partner).start()
    gains = mine[:, chunk:].T[0:1]
    for index, s in enumerate(twins):
        share_copy(0, s, partner).wait_recv()
        share_copy(1 + len(twins) + index, s, partner).start()
    share_copy(0, partner, partner).wait_recv()
    for s in twins:
        share_copy(0, s + 1 - 2 * lax.rem(s, 2), partner).wait_recv()

    first = first + nonlocal_part(0, gains)
    hi_ref[1] = first.astype(BF16)
    for copy in halo_copies(1):
        copy.start()
    second = own_cells(1, first) + nonlocal_part(1, gains)
    second = 2.0 * (second + rims(1)) - start
    hi_ref[2] = second.astype(BF16)
    for copy in halo_copies(2):
        copy.start()
    last = own_cells(2, second) + nonlocal_part(2, gains)
    out_ref[...] = 2.0 * (last + rims(2)) - first

    for d in range(n_states):
        for i in range(tiles):
            if d:
                part_copy(i, d).wait_send()
            else:

                @pl.when(me_s * tiles + i != me_g)
                def _():
                    part_copy(i, 0).wait_send()

    share_copy(0, me_s, partner).wait_send()
    for index, s in enumerate(twins):
        share_copy(1 + index, me_s, s).wait_send()
        share_copy(1 + len(twins) + index, s, partner).wait_send()
    for step in range(3):
        for copy in halo_copies(step):
            copy.wait_send()


def shards(states_in, potential, projectors, proj_gains, atom_owner, atom_rows, wrap_rows):
    _, planes, breadth, depth = states_in.shape
    n_grid, n_states = lax.axis_size("grid"), lax.axis_size("states")
    _, held, nproj, span = projectors.shape
    atoms = atom_owner.shape[0]
    cells, rim = planes * breadth, RADIUS * breadth
    tiles = held // PAIR_CAP
    chunk = span // n_states
    slot_rows = PAIR_CAP * nproj
    inner, low, high, across, centre_weight = stencil_matrices(planes, breadth, depth)
    inner_h, inner_l = halves(inner)
    rim_matrices = np.stack([np.stack(halves(low)), np.stack(halves(high))])
    across_both = np.concatenate(halves(across), axis=1)
    gains = jnp.broadcast_to(proj_gains.reshape(held * nproj, 1), (held * nproj, depth))
    dims = (n_grid, n_states, tiles, chunk, breadth, nproj, atoms, centre_weight)
    vmem = pl.BlockSpec(memory_space=pltpu.VMEM)
    smem = pl.BlockSpec(memory_space=pltpu.SMEM)
    flops = 2 * 3 * depth * cells * (5 * cells + 3 * depth)
    out = pl.pallas_call(
        functools.partial(kernel, dims),
        out_shape=jax.ShapeDtypeStruct((cells, depth), F32),
        in_specs=[vmem, vmem, vmem, vmem, smem, vmem, smem, vmem, vmem, vmem, vmem],
        out_specs=vmem,
        scratch_shapes=[
            pltpu.VMEM((tiles, n_states, slot_rows, chunk + depth), BF16),
            pltpu.VMEM((n_grid, slot_rows, chunk + depth), BF16),
            pltpu.VMEM((n_states, atoms * nproj, chunk), BF16),
            pltpu.VMEM((3, cells, depth), BF16),
            pltpu.VMEM((3, 2, rim, depth), BF16),
            pltpu.VMEM((ATOM_PAD * atom_rows.shape[1], cells), BF16),
            pltpu.VMEM((cells, ATOM_PAD * atom_rows.shape[1]), BF16),
            pltpu.VMEM((2, 2, rim, rim), BF16),
            pltpu.VMEM((cells, depth), F32),
            pltpu.SemaphoreType.DMA((tiles, n_states)),
            pltpu.SemaphoreType.DMA((n_grid,)),
            pltpu.SemaphoreType.DMA((n_states,)),
            pltpu.SemaphoreType.DMA((n_states,)),
            pltpu.SemaphoreType.DMA((3, 2)),
            pltpu.SemaphoreType.DMA((3, 2)),
        ],
        compiler_params=pltpu.CompilerParams(
            collective_id=0, has_side_effects=True, vmem_limit_bytes=40 * 1024 * 1024
        ),
        cost_estimate=pl.CostEstimate(
            flops=flops, bytes_accessed=4 * 1024 * 1024, transcendentals=0
        ),
    )(
        states_in.reshape(cells, depth),
        potential.reshape(cells, depth),
        projectors.reshape(held * nproj, span),
        gains,
        atom_owner,
        atom_rows,
        wrap_rows,
        jnp.asarray(inner_h),
        jnp.asarray(inner_l),
        jnp.asarray(rim_matrices),
        jnp.asarray(across_both),
    )
    return out.reshape(states_in.shape)


def solution(mesh):
    in_specs = (
        P("states", "grid", None, None),
        P("grid", None, None),
        P("grid", "states", None, None),
        P("grid", "states", None),
        P("grid"),
        P("grid", None),
        P(),
    )
    out_specs = P("states", "grid", None, None)
    return jax.shard_map(shards, mesh=mesh, in_specs=in_specs, out_specs=out_specs, check_vma=False)
```

time: 188 us -> 45.5 us (0.24)
  local copies, waits for them, and re-layouts: 76.2 us -> 8.92 us
  starting transfers between devices: 45.1 us -> 0 us
  Pallas kernels: 0 us -> 36.1 us
  other arithmetic: 28.2 us -> 0 us
  between operations: 14.5 us -> 0.02 us
  waiting for transfers between devices: 11.2 us -> 0 us
  matrix products: 6.7 us -> 0 us
  blocking collectives: 5.16 us -> 0 us
    slice x72 -> x0, local copies, waits for them, and re-layouts: 48.5 us -> none  [the longest x33 22.9 us: laplacian(): jnp.roll(padded, k, 2)]
    pallas_call x0 -> x1, Pallas kernels: none -> 36.1 us  [shards(): pl.pallas_call(functools.partial(kernel, dims), out_shape=jax.ShapeDtypeS...]
    all_to_all x6 -> x0, starting transfers between devices: 35 us -> none  [the longest x3 18 us: at_owner(): lax.all_to_all(projected, 'grid', split_axis=0, concat_axis=0, tiled=True)]
    all_to_all x6 -> x0, waiting for transfers between devices: 10.5 us -> none  [the longest x3 10.5 us: at_owner(): lax.all_to_all(projected, 'grid', split_axis=0, concat_axis=0, tiled=True)]
    ppermute x6 -> x0, starting transfers between devices: 10.1 us -> none  [the longest x3 9.14 us: padded_2(): after = lax.ppermute(initial, axis, down)]
    gather x12 -> x0, local copies, waits for them, and re-layouts: 10.1 us -> none  [the longest x3 3.91 us: pick_rows(): jnp.take(lines_here, local_rows, axis=1, mode='fill', fill_value=0.0)]
    add x3 -> x0, other arithmetic: 9.85 us -> none  [laplacian(): y_slope + first_weights[k] * (jnp.roll(padded, -k, 2) - jnp.roll(padded,...]
    sub x2 -> x0, other arithmetic: 7.02 us -> none  [the longest x1 3.7 us: shards(): second_term = 2.0 * shifted(first_term) - states_in]
  transfers between devices with their start and end apart: 13 -> 0, of which waited for: 3 -> 0; matrix products, arithmetic and copies ran while one was open for 30% -> 0% of each run, Pallas kernels for 0% -> 0%
where the time goes in v1:
time: 45.5 us; the launch traced here: 45.1 us
  Pallas kernels  36.1 us (79%)
  local copies, waits for them, and re-layouts  8.92 us (20%)
    pallas_call x1, Pallas kernels, shards(): pl.pallas_call(functools.partial(kernel, dims), out_shape=jax.ShapeDtypeS...  36.1 us
    unnamed x21, local copies, waits for them, and re-layouts  8.07 us

profile of v1, /device:TPU:0, one launch (start us, length us, event | category | flops | bytes accessed | tf_op | source)
XLA Modules:
  0.0 45.1 jit_solution(13654120901209694610)
XLA Ops:
  0.0 0.0 copy-start.3
  0.0 0.8 %broadcast_in_dim.7 = bf16[32]{0:T(256)(128)(2,1)S(1)} reshape(bf16[1,4,8]{2,1,0:T(4,128)(2,1)} %param.14) | data formatting | bytes 128 | tf_op jit(solution)/shard_map/broadcast_in_dim | solution.py:364
  0.8 0.0 copy-start.4
  0.8 0.0 copy-start.5
  0.8 0.1 broadcast_in_dim.8.gain_ref
  0.9 0.0 copy-done.3
  0.9 0.6 %copy-done.4 = s32[10]{0:T(128)S(1)} copy-done((s32[10]{0:T(128)S(1)}, s32[10]{0:T(128)}, u32[]{:S(2)}) %copy-start.4) | copy-done | bytes 64
  1.4 0.0 copy-done.5
  1.5 0.0 copy-start
  1.5 0.9 %copy-done = f32[1,16,32,128]{3,2,1,0:T(8,128)S(1)} copy-done((f32[1,16,32,128]{3,2,1,0:T(8,128)S(1)}, f32[1,16,32,128]{3,2,1,0:T(8,128)}, u32[]{:S(2)}) %copy-start) | copy-done | bytes 262168
  2.4 0.0 copy-start.1
  2.4 0.9 %copy-done.1 = f32[16,32,128]{2,1,0:T(8,128)S(1)} copy-done((f32[16,32,128]{2,1,0:T(8,128)S(1)}, f32[16,32,128]{2,1,0:T(8,128)}, u32[]{:S(2)}) %copy-start.1) | copy-done | bytes 262168
  3.4 0.0 copy-start.2
  3.4 0.9 %copy-done.2 = bf16[1,4,8,4096]{3,2,1,0:T(8,128)(2,1)S(1)} copy-done((bf16[1,4,8,4096]{3,2,1,0:T(8,128)(2,1)S(1)}, bf16[1,4,8,4096]{3,2,1,0:T(8,128)(2,1)}, u32[]{:S(2)}) %copy-start.2) | copy-done | bytes 262168
  4.3 0.0 copy-start.6
  4.3 1.0 %copy-done.6 = bf16[512,512]{1,0:T(8,128)(2,1)S(1)} copy-done((bf16[512,512]{1,0:T(8,128)(2,1)S(1)}, bf16[512,512]{1,0:T(8,128)(2,1)}, u32[]{:S(2)}) %copy-start.6) | copy-done | bytes 524312
  5.3 0.0 copy-start.7
  5.3 1.0 %copy-done.7 = bf16[512,512]{1,0:T(8,128)(2,1)S(1)} copy-done((bf16[512,512]{1,0:T(8,128)(2,1)S(1)}, bf16[512,512]{1,0:T(8,128)(2,1)}, u32[]{:S(2)}) %copy-start.7) | copy-done | bytes 524312
  6.4 0.0 copy-start.8
  6.4 1.0 %copy-done.8 = bf16[2,2,192,192]{3,2,1,0:T(8,128)(2,1)S(1)} copy-done((bf16[2,2,192,192]{3,2,1,0:T(8,128)(2,1)S(1)}, bf16[2,2,192,192]{3,2,1,0:T(8,128)(2,1)}, u32[]{:S(2)}) %copy-start.8) | copy-done | bytes 294936
  7.4 0.0 copy-start.9
  7.4 0.8 %copy-done.9 = bf16[128,256]{1,0:T(8,128)(2,1)S(1)} copy-done((bf16[128,256]{1,0:T(8,128)(2,1)S(1)}, bf16[128,256]{1,0:T(8,128)(2,1)}, u32[]{:S(2)}) %copy-start.9) | copy-done | bytes 65560
  8.2 36.1 %shard_map.109 = f32[512,128]{1,0:T(8,128)S(1)} custom-call(f32[512,128]{1,0:T(8,128)S(1)} %bitcast.5, f32[512,128]{1,0:T(8,128)S(1)} %bitcast.6, bf16[32,4096]{1,0:T(8,128)(2,1)S(1)} %bitcast.7, bf16[32,128]{1,0:T(8,128)(2,1)S(1)} %broadcast_in_dim.8.gain_ref, s32[10]{0:T(128)S(1)} %copy-done.4, s32[10,32]{1,0:T(8,128)S(1)} %copy-done.3, s32[32]{0:T(128)S(1)} %copy-done.5, ...), custom_call_target="tpu_custom_call" | custom-call | flops 1157627904 | bytes 4194304 | tf_op jit(solution)/shard_map/pallas_call | solution.py:369
  44.3 0.7 %copy.13 = f32[1,16,32,128]{3,2,1,0:T(8,128)} copy(f32[1,16,32,128]{3,2,1,0:T(8,128)S(1)} %bitcast.4) | data formatting | bytes 524288
Async XLA Ops:
  0.0 0.9 %copy-start.3 = (s32[10,32]{1,0:T(8,128)S(1)}, s32[10,32]{1,0:T(8,128)}, u32[]{:S(2)}) copy-start(s32[10,32]{1,0:T(8,128)} %rows_ref.1) | copy-start | bytes 3844
  0.8 0.7 %copy-start.4 = (s32[10]{0:T(128)S(1)}, s32[10]{0:T(128)}, u32[]{:S(2)}) copy-start(s32[10]{0:T(128)} %owner_ref.1) | copy-start | bytes 124
  0.8 0.7 %copy-start.5 = (s32[32]{0:T(128)S(1)}, s32[32]{0:T(128)}, u32[]{:S(2)}) copy-start(s32[32]{0:T(128)} %wrap_ref.1) | copy-start | bytes 388
  1.5 0.9 %copy-start = (f32[1,16,32,128]{3,2,1,0:T(8,128)S(1)}, f32[1,16,32,128]{3,2,1,0:T(8,128)}, u32[]{:S(2)}) copy-start(f32[1,16,32,128]{3,2,1,0:T(8,128)} %param.11) | copy-start | bytes 786436
  2.4 0.9 %copy-start.1 = (f32[16,32,128]{2,1,0:T(8,128)S(1)}, f32[16,32,128]{2,1,0:T(8,128)}, u32[]{:S(2)}) copy-start(f32[16,32,128]{2,1,0:T(8,128)} %param.12) | copy-start | bytes 786436
  3.4 0.9 %copy-start.2 = (bf16[1,4,8,4096]{3,2,1,0:T(8,128)(2,1)S(1)}, bf16[1,4,8,4096]{3,2,1,0:T(8,128)(2,1)}, u32[]{:S(2)}) copy-start(bf16[1,4,8,4096]{3,2,1,0:T(8,128)(2,1)} %param.13) | copy-start | bytes 786436
  4.3 1.0 %copy-start.6 = (bf16[512,512]{1,0:T(8,128)(2,1)S(1)}, bf16[512,512]{1,0:T(8,128)(2,1)}, u32[]{:S(2)}) copy-start(bf16[512,512]{1,0:T(8,128)(2,1)} %constant.9.clone.inner_l_ref) | copy-start | bytes 1572868
  5.3 1.0 %copy-start.7 = (bf16[512,512]{1,0:T(8,128)(2,1)S(1)}, bf16[512,512]{1,0:T(8,128)(2,1)}, u32[]{:S(2)}) copy-start(bf16[512,512]{1,0:T(8,128)(2,1)} %constant.8.clone.inner_h_ref) | copy-start | bytes 1572868
  6.4 1.0 %copy-start.8 = (bf16[2,2,192,192]{3,2,1,0:T(8,128)(2,1)S(1)}, bf16[2,2,192,192]{3,2,1,0:T(8,128)(2,1)}, u32[]{:S(2)}) copy-start(bf16[2,2,192,192]{3,2,1,0:T(8,128)(2,1)} %constant.10.clone.rim_ref) | copy-start | bytes 884740
  7.4 0.8 %copy-start.9 = (bf16[128,256]{1,0:T(8,128)(2,1)S(1)}, bf16[128,256]{1,0:T(8,128)(2,1)}, u32[]{:S(2)}) copy-start(bf16[128,256]{1,0:T(8,128)(2,1)} %constant.11.clone.across_ref) | copy-start | bytes 196612

commit v2 on v1

--- a/solution.py
+++ b/solution.py
@@ -13,6 +13,7 @@
 RADIUS = 6
 PAIR_CAP = 2
 ATOM_PAD = 16
+PIECES = 2
 
 MIXED_WEIGHT = 0.7
 CENTER = 12.0
@@ -87,20 +88,28 @@
 
 def kernel(
     dims,
-    v_ref,
-    pot_ref,
-    proj_ref,
+    v_hbm,
+    pot_hbm,
+    proj_hbm,
+    inner_h_hbm,
+    inner_l_hbm,
+    rim_hbm,
+    across_hbm,
     gain_ref,
     owner_ref,
     rows_ref,
     wrap_ref,
+    out_ref,
+    v_ref,
+    pot_ref,
     inner_h_ref,
     inner_l_ref,
     rim_ref,
     across_ref,
-    out_ref,
     sendbuf,
+    sendbuf_last,
     arrived,
+    arrived_last,
     parts,
     hi_ref,
     halo,
@@ -108,6 +117,8 @@
     place_ref,
     rim_turned,
     base_ref,
+    load_sem,
+    piece_sem,
     part_send,
     part_recv,
     share_send,
@@ -118,7 +129,8 @@
     n_grid, n_states, tiles, chunk, breadth, nproj, atoms, centre_weight = dims
     cells, depth = v_ref.shape
     rim = RADIUS * breadth
-    blocks = chunk // depth
+    piece = chunk // PIECES
+    blocks = piece // depth
     slot_rows = PAIR_CAP * nproj
     me_g, me_s = lax.axis_index("grid"), lax.axis_index("states")
     up, down = lax.rem(me_g + 1, n_grid), lax.rem(me_g + n_grid - 1, n_grid)
@@ -126,6 +138,42 @@
     partner = me_s + 1 - 2 * lax.rem(me_s, 2)
     twins = [lax.rem(me_s + 2 * d, n_states) for d in range(1, n_states // 2)]
 
+    def outgoing(h, i, s):
+        return sendbuf_last.at[i, s] if h == PIECES - 1 else sendbuf.at[h, i, s]
+
+    def incoming(h, o):
+        return arrived_last.at[o] if h == PIECES - 1 else arrived.at[h, o]
+
+    piece_loads = [
+        pltpu.make_async_copy(
+            proj_hbm.at[pl.ds(i * slot_rows, slot_rows), pl.ds(s * chunk + h * piece, piece)],
+            outgoing(h, i, s).at[:, pl.ds(0, piece)],
+            piece_sem.at[h, i, s],
+        )
+        for h in range(PIECES)
+        for i in range(tiles)
+        for s in range(n_states)
+    ]
+    load_v, load_pot, *load_tables = [
+        pltpu.make_async_copy(src, dst, load_sem.at[n])
+        for n, (src, dst) in enumerate(
+            (
+                (v_hbm, v_ref),
+                (pot_hbm, pot_ref),
+                (inner_h_hbm, inner_h_ref),
+                (inner_l_hbm, inner_l_ref),
+                (rim_hbm, rim_ref),
+                (across_hbm, across_ref),
+            )
+        )
+    ]
+    load_v.start()
+    for load in piece_loads:
+        load.start()
+    load_pot.start()
+    for load in load_tables:
+        load.start()
+
     barrier = pltpu.get_barrier_semaphore()
 
     def greet(g, s):
@@ -143,22 +191,28 @@
     for s in twins:
         greet(me_g, s)
 
+    gain_rows = gain_ref[...]
+    nothing = jnp.zeros((slot_rows, depth - nproj), BF16)
+    below = jnp.zeros((slot_rows - PAIR_CAP, nproj), BF16)
     for i in range(tiles):
-        held = pl.ds(i * slot_rows, slot_rows)
+        own_rows = gain_rows[i * PAIR_CAP : (i + 1) * PAIR_CAP]
+        block = jnp.concatenate([jnp.concatenate([own_rows, below], axis=0), nothing], axis=1)
         for s in range(n_states):
-            sendbuf[i, s, :, :chunk] = proj_ref[held, s * chunk : (s + 1) * chunk]
-            sendbuf[i, s, :, chunk:] = gain_ref[held, :]
+            sendbuf_last[i, s, :, piece:] = block
+    load_v.wait()
     hi_ref[0] = v_ref[...].astype(BF16)
+    for load in piece_loads:
+        load.wait()
 
     pl.semaphore_wait(barrier, n_grid + 2 + len(twins) + jnp.where(holder == me_s, 0, 1))
 
-    def part_copy(i, d):
+    def part_copy(h, i, d):
         s = lax.rem(me_s + d, n_states)
         return pltpu.make_async_remote_copy(
-            src_ref=sendbuf.at[i, s],
-            dst_ref=arrived.at[me_g],
-            send_sem=part_send.at[i, d],
-            recv_sem=part_recv.at[me_g],
+            src_ref=outgoing(h, i, s),
+            dst_ref=incoming(h, me_g),
+            send_sem=part_send.at[h, i, d],
+            recv_sem=part_recv.at[h, me_g],
             device_id=(me_s * tiles + i, s),
             device_id_type=MESH,
         )
@@ -176,29 +230,30 @@
             for side, start, target in ((0, cells - rim, up), (1, 0, down))
         ]
 
-    def share_copy(index, part, target):
+    def share_copy(h, index, part, target):
         return pltpu.make_async_remote_copy(
-            src_ref=parts.at[part],
-            dst_ref=parts.at[part],
-            send_sem=share_send.at[index],
-            recv_sem=share_recv.at[part],
+            src_ref=parts.at[part, h],
+            dst_ref=parts.at[part, h],
+            send_sem=share_send.at[h, index],
+            recv_sem=share_recv.at[h, part],
             device_id=(me_g, target),
             device_id_type=MESH,
         )
 
-    for d in range(n_states - 1, -1, -1):
-        for i in range(tiles):
-            if d:
-                part_copy(i, d).start()
-            else:
-
-                @pl.when(me_s * tiles + i != me_g)
-                def _():
-                    part_copy(i, 0).start()
-
-                @pl.when(me_s * tiles + i == me_g)
-                def _():
-                    arrived[me_g] = sendbuf[i, me_s]
+    for h in range(PIECES):
+        for d in range(n_states - 1, -1, -1):
+            for i in range(tiles):
+                if d:
+                    part_copy(h, i, d).start()
+                else:
+
+                    @pl.when(me_s * tiles + i != me_g)
+                    def _():
+                        part_copy(h, i, 0).start()
+
+                    @pl.when(me_s * tiles + i == me_g)
+                    def _():
+                        incoming(h, me_g)[...] = outgoing(h, i, me_s)[...]
 
     for copy in halo_copies(0):
         copy.start()
@@ -217,6 +272,19 @@
         [jnp.where(lane == slots[a] * nproj + row, 1.0, 0.0) for a in range(atoms)], axis=0
     ).astype(BF16)
 
+    lane = lax.broadcasted_iota(jnp.int32, (1, width), 1)
+    places = [(slot // PAIR_CAP) * slot_rows + lax.rem(slot, PAIR_CAP) for slot in slots]
+    slot_lines = [jnp.where(lane == place, 1.0, 0.0) for place in places]
+    slot_lines = jnp.concatenate(
+        slot_lines + [jnp.zeros((ATOM_PAD - atoms, width), F32)], axis=0
+    ).astype(BF16)
+    spread = jnp.where(
+        lax.rem(lax.broadcasted_iota(jnp.int32, (depth, atoms * nproj), 1), nproj)
+        == lax.broadcasted_iota(jnp.int32, (depth, atoms * nproj), 0),
+        1.0,
+        0.0,
+    ).astype(BF16)
+
     block_rows = rows_ref.shape[1]
     local = rows_ref[...] - me_g * cells
     local = jnp.concatenate(
@@ -229,6 +297,10 @@
     pick_ref[...] = pick.astype(BF16)
     place_ref[...] = pick.T.astype(BF16)
 
+    load_pot.wait()
+    for load in load_tables:
+        load.wait()
+
     turn = wrap_ref[0]
     source = lax.broadcasted_iota(jnp.int32, (rim, rim), 0)
     target = lax.broadcasted_iota(jnp.int32, (rim, rim), 1)
@@ -267,14 +339,15 @@
     def nonlocal_part(step, gains):
         picked = dot(pick_ref[...], hi_ref[step]).astype(BF16)
         coefficients = jnp.zeros((ATOM_PAD, atoms * nproj), F32)
-        for q in range(n_states):
+        pairs = [(q, h) for q in range(n_states) for h in range(PIECES)]
+        for n, (q, h) in enumerate(pairs):
             lines = [
-                picked[(q * blocks + b) * ATOM_PAD : (q * blocks + b + 1) * ATOM_PAD]
-                for b in range(blocks)
+                picked[b * ATOM_PAD : (b + 1) * ATOM_PAD]
+                for b in range(n * blocks, (n + 1) * blocks)
             ]
             coefficients = coefficients + lax.dot_general(
                 jnp.concatenate(lines, axis=1),
-                parts[q],
+                parts[q, h],
                 (((1,), (1,)), ((), ())),
                 preferred_element_type=F32,
             )
@@ -282,8 +355,8 @@
         column = lax.broadcasted_iota(jnp.int32, coefficients.shape, 1)
         scaled = jnp.where(column // nproj == atom, coefficients * gains, 0.0).astype(BF16)
         pieces = []
-        for q in range(n_states):
-            projected = dot(scaled, parts[q]).astype(BF16)
+        for q, h in pairs:
+            projected = dot(scaled, parts[q, h]).astype(BF16)
             pieces += [projected[:, b * depth : (b + 1) * depth] for b in range(blocks)]
         return dot(place_ref[...], jnp.concatenate(pieces, axis=0)) * (1.0 / HALF_WIDTH)
 
@@ -291,31 +364,41 @@
     first = own_cells(0, start)
     first = first + rims(0)
 
-    for o in range(n_grid):
-
-        @pl.when((me_g != o) | (holder != me_s))
-        def _():
-            pltpu.make_async_remote_copy(
-                src_ref=sendbuf.at[0, 0],
-                dst_ref=arrived.at[o],
-                send_sem=part_send.at[0, 0],
-                recv_sem=part_recv.at[o],
-                device_id=(o, holder),
-                device_id_type=MESH,
-            ).wait_recv()
-
-    mine = dot(chosen, arrived[...].reshape(width, chunk + depth))
-    parts[me_s] = mine[:, :chunk].astype(BF16)
-    for index, s in enumerate(twins):
-        share_copy(1 + index, me_s, s).start()
-    share_copy(0, me_s, partner).start()
-    gains = mine[:, chunk:].T[0:1]
-    for index, s in enumerate(twins):
-        share_copy(0, s, partner).wait_recv()
-        share_copy(1 + len(twins) + index, s, partner).start()
-    share_copy(0, partner, partner).wait_recv()
-    for s in twins:
-        share_copy(0, s + 1 - 2 * lax.rem(s, 2), partner).wait_recv()
+    def forward(h):
+        for index, s in enumerate(twins):
+            share_copy(h, 0, s, partner).wait_recv()
+            share_copy(h, 1 + len(twins) + index, s, partner).start()
+
+    for h in range(PIECES):
+        for o in range(n_grid):
+
+            @pl.when((me_g != o) | (holder != me_s))
+            def _():
+                pltpu.make_async_remote_copy(
+                    src_ref=outgoing(h, 0, 0),
+                    dst_ref=incoming(h, o),
+                    send_sem=part_send.at[h, 0, 0],
+                    recv_sem=part_recv.at[h, o],
+                    device_id=(o, holder),
+                    device_id_type=MESH,
+                ).wait_recv()
+
+        if h == PIECES - 1:
+            came = arrived_last[...].reshape(width, piece + depth)
+            parts[me_s, h] = dot(chosen, came[:, :piece]).astype(BF16)
+        else:
+            parts[me_s, h] = dot(chosen, arrived[h].reshape(width, piece)).astype(BF16)
+        for index, s in enumerate(twins):
+            share_copy(h, 1 + index, me_s, s).start()
+        share_copy(h, 0, me_s, partner).start()
+        if h:
+            forward(h - 1)
+    gains = dot(dot(slot_lines, came[:, piece:]).astype(BF16), spread)
+    forward(PIECES - 1)
+    for h in range(PIECES):
+        share_copy(h, 0, partner, partner).wait_recv()
+        for s in twins:
+            share_copy(h, 0, s + 1 - 2 * lax.rem(s, 2), partner).wait_recv()
 
     first = first + nonlocal_part(0, gains)
     hi_ref[1] = first.astype(BF16)
@@ -329,20 +412,21 @@
     last = own_cells(2, second) + nonlocal_part(2, gains)
     out_ref[...] = 2.0 * (last + rims(2)) - first
 
-    for d in range(n_states):
-        for i in range(tiles):
-            if d:
-                part_copy(i, d).wait_send()
-            else:
-
-                @pl.when(me_s * tiles + i != me_g)
-                def _():
-                    part_copy(i, 0).wait_send()
-
-    share_copy(0, me_s, partner).wait_send()
-    for index, s in enumerate(twins):
-        share_copy(1 + index, me_s, s).wait_send()
-        share_copy(1 + len(twins) + index, s, partner).wait_send()
+    for h in range(PIECES):
+        for d in range(n_states):
+            for i in range(tiles):
+                if d:
+                    part_copy(h, i, d).wait_send()
+                else:
+
+                    @pl.when(me_s * tiles + i != me_g)
+                    def _():
+                        part_copy(h, i, 0).wait_send()
+
+        share_copy(h, 0, me_s, partner).wait_send()
+        for index, s in enumerate(twins):
+            share_copy(h, 1 + index, me_s, s).wait_send()
+            share_copy(h, 1 + len(twins) + index, s, partner).wait_send()
     for step in range(3):
         for copy in halo_copies(step):
             copy.wait_send()
@@ -356,40 +440,51 @@
     cells, rim = planes * breadth, RADIUS * breadth
     tiles = held // PAIR_CAP
     chunk = span // n_states
+    piece = chunk // PIECES
     slot_rows = PAIR_CAP * nproj
     inner, low, high, across, centre_weight = stencil_matrices(planes, breadth, depth)
     inner_h, inner_l = halves(inner)
     rim_matrices = np.stack([np.stack(halves(low)), np.stack(halves(high))])
     across_both = np.concatenate(halves(across), axis=1)
-    gains = jnp.broadcast_to(proj_gains.reshape(held * nproj, 1), (held * nproj, depth))
     dims = (n_grid, n_states, tiles, chunk, breadth, nproj, atoms, centre_weight)
+    hbm = pl.BlockSpec(memory_space=pltpu.HBM)
     vmem = pl.BlockSpec(memory_space=pltpu.VMEM)
     smem = pl.BlockSpec(memory_space=pltpu.SMEM)
     flops = 2 * 3 * depth * cells * (5 * cells + 3 * depth)
     out = pl.pallas_call(
         functools.partial(kernel, dims),
         out_shape=jax.ShapeDtypeStruct((cells, depth), F32),
-        in_specs=[vmem, vmem, vmem, vmem, smem, vmem, smem, vmem, vmem, vmem, vmem],
+        in_specs=[hbm] * 7 + [vmem, smem, vmem, smem],
         out_specs=vmem,
         scratch_shapes=[
-            pltpu.VMEM((tiles, n_states, slot_rows, chunk + depth), BF16),
-            pltpu.VMEM((n_grid, slot_rows, chunk + depth), BF16),
-            pltpu.VMEM((n_states, atoms * nproj, chunk), BF16),
+            pltpu.VMEM((cells, depth), F32),
+            pltpu.VMEM((cells, depth), F32),
+            pltpu.VMEM((cells, cells), BF16),
+            pltpu.VMEM((cells, cells), BF16),
+            pltpu.VMEM((2, 2, rim, rim), BF16),
+            pltpu.VMEM((depth, 2 * depth), BF16),
+            pltpu.VMEM((PIECES - 1, tiles, n_states, slot_rows, piece), BF16),
+            pltpu.VMEM((tiles, n_states, slot_rows, piece + depth), BF16),
+            pltpu.VMEM((PIECES - 1, n_grid, slot_rows, piece), BF16),
+            pltpu.VMEM((n_grid, slot_rows, piece + depth), BF16),
+            pltpu.VMEM((n_states, PIECES, atoms * nproj, piece), BF16),
             pltpu.VMEM((3, cells, depth), BF16),
             pltpu.VMEM((3, 2, rim, depth), BF16),
             pltpu.VMEM((ATOM_PAD * atom_rows.shape[1], cells), BF16),
             pltpu.VMEM((cells, ATOM_PAD * atom_rows.shape[1]), BF16),
             pltpu.VMEM((2, 2, rim, rim), BF16),
             pltpu.VMEM((cells, depth), F32),
-            pltpu.SemaphoreType.DMA((tiles, n_states)),
-            pltpu.SemaphoreType.DMA((n_grid,)),
-            pltpu.SemaphoreType.DMA((n_states,)),
-            pltpu.SemaphoreType.DMA((n_states,)),
+            pltpu.SemaphoreType.DMA((6,)),
+            pltpu.SemaphoreType.DMA((PIECES, tiles, n_states)),
+            pltpu.SemaphoreType.DMA((PIECES, tiles, n_states)),
+            pltpu.SemaphoreType.DMA((PIECES, n_grid)),
+            pltpu.SemaphoreType.DMA((PIECES, n_states)),
+            pltpu.SemaphoreType.DMA((PIECES, n_states)),
             pltpu.SemaphoreType.DMA((3, 2)),
             pltpu.SemaphoreType.DMA((3, 2)),
         ],
         compiler_params=pltpu.CompilerParams(
-            collective_id=0, has_side_effects=True, vmem_limit_bytes=40 * 1024 * 1024
+            collective_id=0, has_side_effects=True, vmem_limit_bytes=63 * 1024 * 1024
         ),
         cost_estimate=pl.CostEstimate(
             flops=flops, bytes_accessed=4 * 1024 * 1024, transcendentals=0
@@ -398,14 +493,14 @@
         states_in.reshape(cells, depth),
         potential.reshape(cells, depth),
         projectors.reshape(held * nproj, span),
-        gains,
-        atom_owner,
-        atom_rows,
-        wrap_rows,
         jnp.asarray(inner_h),
         jnp.asarray(inner_l),
         jnp.asarray(rim_matrices),
         jnp.asarray(across_both),
+        proj_gains.reshape(held, nproj),
+        atom_owner,
+        atom_rows,
+        wrap_rows,
     )
     return out.reshape(states_in.shape)
 

time: 45.5 us -> 39.6 us (0.87)
  local copies, waits for them, and re-layouts: 8.92 us -> 1.67 us
  Pallas kernels: 36.1 us -> 37.7 us
    unnamed x21 -> x1, local copies, waits for them, and re-layouts: 8.07 us -> 1.67 us
    pallas_call x1, Pallas kernels: 36.1 us -> 37.7 us  [shards(): pl.pallas_call(functools.partial(kernel, dims), out_shape=jax.ShapeDtypeS...]
    broadcast_in_dim x2 -> x0, local copies, waits for them, and re-layouts: 0.85 us -> none  [shards(): jnp.broadcast_to(proj_gains.reshape(held * nproj, 1), (held * nproj, depth))]
where the time goes in v2:
time: 39.6 us; the launch traced here: 39.4 us
  Pallas kernels  37.7 us (95%)
  local copies, waits for them, and re-layouts  1.67 us (4%)
    pallas_call x1, Pallas kernels, shards(): pl.pallas_call(functools.partial(kernel, dims), out_shape=jax.ShapeDtypeS...  37.7 us
    unnamed x1, local copies, waits for them, and re-layouts  1.67 us

profile of v2, /device:TPU:0, one launch (start us, length us, event | category | flops | bytes accessed | tf_op | source)
XLA Modules:
  0.0 39.4 jit_solution(1841125911919152263)
XLA Ops:
  0.0 37.7 %shard_map.109 = f32[512,128]{1,0:T(8,128)} custom-call(f32[512,128]{1,0:T(8,128)} %bitcast.6, f32[512,128]{1,0:T(8,128)} %bitcast.7, bf16[32,4096]{1,0:T(8,128)(2,1)} %bitcast.8, bf16[512,512]{1,0:T(8,128)(2,1)} %constant.8.clone.inner_h_hbm, bf16[512,512]{1,0:T(8,128)(2,1)} %constant.9.clone.inner_l_hbm, bf16[2,2,192,192]{3,2,1,0:T(8,128)(2,1)} %constant.10.clone.rim_hbm, ...), custom_call_target="tpu_custom_call" | custom-call | flops 1157627904 | bytes 4194304 | tf_op jit(solution)/shard_map/pallas_call | solution.py:454
  37.7 1.7 %copy.13 = f32[1,16,32,128]{3,2,1,0:T(8,128)} copy(f32[1,16,32,128]{3,2,1,0:T(8,128)} %bitcast.5) | data formatting | bytes 524288

commit v3 on v2

--- a/solution.py
+++ b/solution.py
@@ -128,6 +128,7 @@
 ):
     n_grid, n_states, tiles, chunk, breadth, nproj, atoms, centre_weight = dims
     cells, depth = v_ref.shape
+    breadth_bits, proj_bits = breadth.bit_length() - 1, nproj.bit_length() - 1
     rim = RADIUS * breadth
     piece = chunk // PIECES
     blocks = piece // depth
@@ -259,12 +260,13 @@
         copy.start()
 
     owners = [owner_ref[a] for a in range(atoms)]
-    slots = []
+    slots, ranks = [], []
     for a in range(atoms):
         rank = jnp.int32(0)
         for b in range(a):
             rank = rank + jnp.where(owners[b] == owners[a], 1, 0)
         slots.append(owners[a] * PAIR_CAP + rank)
+        ranks.append(rank)
     width = n_grid * slot_rows
     lane = lax.broadcasted_iota(jnp.int32, (nproj, width), 1)
     row = lax.broadcasted_iota(jnp.int32, (nproj, width), 0)
@@ -273,13 +275,13 @@
     ).astype(BF16)
 
     lane = lax.broadcasted_iota(jnp.int32, (1, width), 1)
-    places = [(slot // PAIR_CAP) * slot_rows + lax.rem(slot, PAIR_CAP) for slot in slots]
+    places = [owner * slot_rows + rank for owner, rank in zip(owners, ranks)]
     slot_lines = [jnp.where(lane == place, 1.0, 0.0) for place in places]
     slot_lines = jnp.concatenate(
         slot_lines + [jnp.zeros((ATOM_PAD - atoms, width), F32)], axis=0
     ).astype(BF16)
     spread = jnp.where(
-        lax.rem(lax.broadcasted_iota(jnp.int32, (depth, atoms * nproj), 1), nproj)
+        (lax.broadcasted_iota(jnp.int32, (depth, atoms * nproj), 1) & (nproj - 1))
         == lax.broadcasted_iota(jnp.int32, (depth, atoms * nproj), 0),
         1.0,
         0.0,
@@ -295,25 +297,6 @@
         [jnp.where(local[:, b : b + 1] == line, 1.0, 0.0) for b in range(block_rows)], axis=0
     )
     pick_ref[...] = pick.astype(BF16)
-    place_ref[...] = pick.T.astype(BF16)
-
-    load_pot.wait()
-    for load in load_tables:
-        load.wait()
-
-    turn = wrap_ref[0]
-    source = lax.broadcasted_iota(jnp.int32, (rim, rim), 0)
-    target = lax.broadcasted_iota(jnp.int32, (rim, rim), 1)
-    low_turn = jnp.where(me_g == 0, turn, 0)
-    high_turn = jnp.where(me_g == n_grid - 1, breadth - turn, 0)
-    for side, shift in ((0, low_turn), (1, high_turn)):
-        same_plane = (source // breadth) == (target // breadth)
-        moved = lax.rem(lax.rem(source, breadth) + shift, breadth) == lax.rem(target, breadth)
-        permute = jnp.where(same_plane & moved, 1.0, 0.0).astype(BF16)
-        for half in range(2):
-            rim_turned[side, half] = dot(rim_ref[side, half], permute).astype(BF16)
-
-    base_ref[...] = (pot_ref[...] - CENTER) * (1.0 / HALF_WIDTH) + centre_weight
 
     def own_cells(step, field):
         hi = hi_ref[step]
@@ -353,23 +336,19 @@
             )
         atom = lax.broadcasted_iota(jnp.int32, coefficients.shape, 0)
         column = lax.broadcasted_iota(jnp.int32, coefficients.shape, 1)
-        scaled = jnp.where(column // nproj == atom, coefficients * gains, 0.0).astype(BF16)
+        scaled = jnp.where((column >> proj_bits) == atom, coefficients * gains, 0.0).astype(BF16)
         pieces = []
         for q, h in pairs:
             projected = dot(scaled, parts[q, h]).astype(BF16)
             pieces += [projected[:, b * depth : (b + 1) * depth] for b in range(blocks)]
         return dot(place_ref[...], jnp.concatenate(pieces, axis=0)) * (1.0 / HALF_WIDTH)
 
-    start = v_ref[...]
-    first = own_cells(0, start)
-    first = first + rims(0)
-
     def forward(h):
         for index, s in enumerate(twins):
             share_copy(h, 0, s, partner).wait_recv()
             share_copy(h, 1 + len(twins) + index, s, partner).start()
 
-    for h in range(PIECES):
+    def take_share(h):
         for o in range(n_grid):
 
             @pl.when((me_g != o) | (holder != me_s))
@@ -383,18 +362,43 @@
                     device_id_type=MESH,
                 ).wait_recv()
 
-        if h == PIECES - 1:
-            came = arrived_last[...].reshape(width, piece + depth)
-            parts[me_s, h] = dot(chosen, came[:, :piece]).astype(BF16)
-        else:
-            parts[me_s, h] = dot(chosen, arrived[h].reshape(width, piece)).astype(BF16)
+        last = h == PIECES - 1
+        came = arrived_last[:, :, :piece] if last else arrived[h]
+        parts[me_s, h] = dot(chosen, came.reshape(width, piece)).astype(BF16)
         for index, s in enumerate(twins):
             share_copy(h, 1 + index, me_s, s).start()
         share_copy(h, 0, me_s, partner).start()
-        if h:
-            forward(h - 1)
-    gains = dot(dot(slot_lines, came[:, piece:]).astype(BF16), spread)
+
+    take_share(0)
+    place_ref[...] = pick.T.astype(BF16)
+    for h in range(1, PIECES):
+        take_share(h)
+    load_pot.wait()
+    for load in load_tables:
+        load.wait()
+
+    turn = wrap_ref[0]
+    source = lax.broadcasted_iota(jnp.int32, (rim, rim), 0)
+    target = lax.broadcasted_iota(jnp.int32, (rim, rim), 1)
+    low_turn = jnp.where(me_g == 0, turn, 0)
+    high_turn = jnp.where(me_g == n_grid - 1, breadth - turn, 0)
+    for side, shift in ((0, low_turn), (1, high_turn)):
+        same_plane = (source >> breadth_bits) == (target >> breadth_bits)
+        moved = ((source + shift) & (breadth - 1)) == (target & (breadth - 1))
+        permute = jnp.where(same_plane & moved, 1.0, 0.0).astype(BF16)
+        for half in range(2):
+            rim_turned[side, half] = dot(rim_ref[side, half], permute).astype(BF16)
+
+    base_ref[...] = (pot_ref[...] - CENTER) * (1.0 / HALF_WIDTH) + centre_weight
+
+    for h in range(PIECES - 1):
+        forward(h)
+    start = v_ref[...]
+    first = own_cells(0, start)
     forward(PIECES - 1)
+    first = first + rims(0)
+    gain_lines = arrived_last[:, :, piece:].reshape(width, depth)
+    gains = dot(dot(slot_lines, gain_lines).astype(BF16), spread)
     for h in range(PIECES):
         share_copy(h, 0, partner, partner).wait_recv()
         for s in twins:

time: 39.6 us -> 39.4 us (level)
  no operation moved by 1% of the time
where the time goes in v3:
time: 39.4 us; the launch traced here: 39.2 us
  Pallas kernels  37.5 us (95%)
  local copies, waits for them, and re-layouts  1.67 us (4%)
    pallas_call x1, Pallas kernels, shards(): pl.pallas_call(functools.partial(kernel, dims), out_shape=jax.ShapeDtypeS...  37.5 us
    unnamed x1, local copies, waits for them, and re-layouts  1.67 us

profile of v3, /device:TPU:0, one launch (start us, length us, event | category | flops | bytes accessed | tf_op | source)
XLA Modules:
  0.0 39.2 jit_solution(278612517355345639)
XLA Ops:
  0.0 37.5 %shard_map.109 = f32[512,128]{1,0:T(8,128)} custom-call(f32[512,128]{1,0:T(8,128)} %bitcast.6, f32[512,128]{1,0:T(8,128)} %bitcast.7, bf16[32,4096]{1,0:T(8,128)(2,1)} %bitcast.8, bf16[512,512]{1,0:T(8,128)(2,1)} %constant.8.clone.inner_h_hbm, bf16[512,512]{1,0:T(8,128)(2,1)} %constant.9.clone.inner_l_hbm, bf16[2,2,192,192]{3,2,1,0:T(8,128)(2,1)} %constant.10.clone.rim_hbm, ...), custom_call_target="tpu_custom_call" | custom-call | flops 1157627904 | bytes 4194304 | tf_op jit(solution)/shard_map/pallas_call | solution.py:458
  37.5 1.7 %copy.13 = f32[1,16,32,128]{3,2,1,0:T(8,128)} copy(f32[1,16,32,128]{3,2,1,0:T(8,128)} %bitcast.5) | data formatting | bytes 524288

commit v4 on v3

--- a/solution.py
+++ b/solution.py
@@ -108,6 +108,8 @@
     across_ref,
     sendbuf,
     sendbuf_last,
+    relay,
+    relay_last,
     arrived,
     arrived_last,
     parts,
@@ -119,6 +121,8 @@
     base_ref,
     load_sem,
     piece_sem,
+    hop_send,
+    hop_recv,
     part_send,
     part_recv,
     share_send,
@@ -135,12 +139,24 @@
     slot_rows = PAIR_CAP * nproj
     me_g, me_s = lax.axis_index("grid"), lax.axis_index("states")
     up, down = lax.rem(me_g + 1, n_grid), lax.rem(me_g + n_grid - 1, n_grid)
-    holder = me_g // tiles
+    core = lax.rem(me_s, 2)
+    side_x, sides = me_s // 2, n_states // 2
+    source_s = 2 * side_x + lax.rem(me_g // tiles, 2)
+    others = [lax.rem(side_x + d, sides) for d in range(1, sides)]
     partner = me_s + 1 - 2 * lax.rem(me_s, 2)
     twins = [lax.rem(me_s + 2 * d, n_states) for d in range(1, n_states // 2)]
 
-    def outgoing(h, i, s):
-        return sendbuf_last.at[i, s] if h == PIECES - 1 else sendbuf.at[h, i, s]
+    def start_copy(copy):
+        copy.start()
+
+    def await_sent(copy):
+        copy.wait_send()
+
+    def outgoing(h, x):
+        return sendbuf_last.at[x] if h == PIECES - 1 else sendbuf.at[h, x]
+
+    def relayed(h, x):
+        return relay_last.at[x] if h == PIECES - 1 else relay.at[h, x]
 
     def incoming(h, o):
         return arrived_last.at[o] if h == PIECES - 1 else arrived.at[h, o]
@@ -148,7 +164,7 @@
     piece_loads = [
         pltpu.make_async_copy(
             proj_hbm.at[pl.ds(i * slot_rows, slot_rows), pl.ds(s * chunk + h * piece, piece)],
-            outgoing(h, i, s).at[:, pl.ds(0, piece)],
+            outgoing(h, s // 2).at[i, s % 2, :, pl.ds(0, piece)],
             piece_sem.at[h, i, s],
         )
         for h in range(PIECES)
@@ -182,9 +198,9 @@
 
     for o in range(n_grid):
 
-        @pl.when((me_g != o) | (holder != me_s))
+        @pl.when((me_g != o) | (source_s != me_s))
         def _():
-            greet(o, holder)
+            greet(o, source_s)
 
     greet(up, me_s)
     greet(down, me_s)
@@ -199,24 +215,59 @@
         own_rows = gain_rows[i * PAIR_CAP : (i + 1) * PAIR_CAP]
         block = jnp.concatenate([jnp.concatenate([own_rows, below], axis=0), nothing], axis=1)
         for s in range(n_states):
-            sendbuf_last[i, s, :, piece:] = block
+            sendbuf_last[s // 2, i, s % 2, :, piece:] = block
     load_v.wait()
     hi_ref[0] = v_ref[...].astype(BF16)
     for load in piece_loads:
         load.wait()
 
-    pl.semaphore_wait(barrier, n_grid + 2 + len(twins) + jnp.where(holder == me_s, 0, 1))
-
-    def part_copy(h, i, d):
-        s = lax.rem(me_s + d, n_states)
+    pl.semaphore_wait(barrier, n_grid + 2 + len(twins) + jnp.where(source_s == me_s, 0, 1))
+
+    def hop_copy(h, d):
         return pltpu.make_async_remote_copy(
-            src_ref=outgoing(h, i, s),
-            dst_ref=incoming(h, me_g),
-            send_sem=part_send.at[h, i, d],
-            recv_sem=part_recv.at[h, me_g],
-            device_id=(me_s * tiles + i, s),
+            src_ref=outgoing(h, others[d]),
+            dst_ref=relayed(h, side_x),
+            send_sem=hop_send.at[h, d],
+            recv_sem=hop_recv.at[h, side_x],
+            device_id=(me_g, 2 * others[d] + core),
             device_id_type=MESH,
         )
+
+    def await_hop(h, d):
+        pltpu.make_async_remote_copy(
+            src_ref=outgoing(h, others[d]),
+            dst_ref=relayed(h, others[d]),
+            send_sem=hop_send.at[h, d],
+            recv_sem=hop_recv.at[h, others[d]],
+            device_id=(me_g, 2 * others[d] + core),
+            device_id_type=MESH,
+        ).wait_recv()
+
+    def part_copies(h, d, act):
+        x = others[d - 1] if d else side_x
+        held = relayed(h, x) if d else outgoing(h, x)
+        for i in range(tiles):
+            tile = (2 * x + core) * tiles + i
+            for c in (1, 0):
+                copy = pltpu.make_async_remote_copy(
+                    src_ref=held.at[i, c],
+                    dst_ref=incoming(h, me_g),
+                    send_sem=part_send.at[h, d, i, c],
+                    recv_sem=part_recv.at[h, me_g],
+                    device_id=(tile, 2 * side_x + c),
+                    device_id_type=MESH,
+                )
+                here = (tile == me_g) & (core == c)
+
+                @pl.when(jnp.logical_not(here))
+                def _():
+                    act(copy)
+
+                if act is start_copy:
+
+                    @pl.when(here)
+                    def _():
+                        incoming(h, me_g)[...] = held[i, c]
 
     def halo_copies(step):
         return [
@@ -242,22 +293,9 @@
         )
 
     for h in range(PIECES):
-        for d in range(n_states - 1, -1, -1):
-            for i in range(tiles):
-                if d:
-                    part_copy(h, i, d).start()
-                else:
-
-                    @pl.when(me_s * tiles + i != me_g)
-                    def _():
-                        part_copy(h, i, 0).start()
-
-                    @pl.when(me_s * tiles + i == me_g)
-                    def _():
-                        incoming(h, me_g)[...] = outgoing(h, i, me_s)[...]
-
-    for copy in halo_copies(0):
-        copy.start()
+        for d in range(sides - 1):
+            hop_copy(h, d).start()
+        part_copies(h, 0, start_copy)
 
     owners = [owner_ref[a] for a in range(atoms)]
     slots, ranks = [], []
@@ -297,6 +335,14 @@
         [jnp.where(local[:, b : b + 1] == line, 1.0, 0.0) for b in range(block_rows)], axis=0
     )
     pick_ref[...] = pick.astype(BF16)
+
+    for h in range(PIECES):
+        for d in range(sides - 1):
+            await_hop(h, d)
+            part_copies(h, d + 1, start_copy)
+    for copy in halo_copies(0):
+        copy.start()
+
 
     def own_cells(step, field):
         hi = hi_ref[step]
@@ -351,14 +397,14 @@
     def take_share(h):
         for o in range(n_grid):
 
-            @pl.when((me_g != o) | (holder != me_s))
+            @pl.when((me_g != o) | (source_s != me_s))
             def _():
                 pltpu.make_async_remote_copy(
-                    src_ref=outgoing(h, 0, 0),
+                    src_ref=outgoing(h, 0).at[0, 0],
                     dst_ref=incoming(h, o),
-                    send_sem=part_send.at[h, 0, 0],
+                    send_sem=part_send.at[h, 0, 0, 0],
                     recv_sem=part_recv.at[h, o],
-                    device_id=(o, holder),
+                    device_id=(o, source_s),
                     device_id_type=MESH,
                 ).wait_recv()
 
@@ -417,16 +463,10 @@
     out_ref[...] = 2.0 * (last + rims(2)) - first
 
     for h in range(PIECES):
-        for d in range(n_states):
-            for i in range(tiles):
-                if d:
-                    part_copy(h, i, d).wait_send()
-                else:
-
-                    @pl.when(me_s * tiles + i != me_g)
-                    def _():
-                        part_copy(h, i, 0).wait_send()
-
+        for d in range(sides - 1):
+            hop_copy(h, d).wait_send()
+        for d in range(sides):
+            part_copies(h, d, await_sent)
         share_copy(h, 0, me_s, partner).wait_send()
         for index, s in enumerate(twins):
             share_copy(h, 1 + index, me_s, s).wait_send()
@@ -444,7 +484,7 @@
     cells, rim = planes * breadth, RADIUS * breadth
     tiles = held // PAIR_CAP
     chunk = span // n_states
-    piece = chunk // PIECES
+    piece, sides = chunk // PIECES, n_states // 2
     slot_rows = PAIR_CAP * nproj
     inner, low, high, across, centre_weight = stencil_matrices(planes, breadth, depth)
     inner_h, inner_l = halves(inner)
@@ -467,8 +507,10 @@
             pltpu.VMEM((cells, cells), BF16),
             pltpu.VMEM((2, 2, rim, rim), BF16),
             pltpu.VMEM((depth, 2 * depth), BF16),
-            pltpu.VMEM((PIECES - 1, tiles, n_states, slot_rows, piece), BF16),
-            pltpu.VMEM((tiles, n_states, slot_rows, piece + depth), BF16),
+            pltpu.VMEM((PIECES - 1, sides, tiles, 2, slot_rows, piece), BF16),
+            pltpu.VMEM((sides, tiles, 2, slot_rows, piece + depth), BF16),
+            pltpu.VMEM((PIECES - 1, sides, tiles, 2, slot_rows, piece), BF16),
+            pltpu.VMEM((sides, tiles, 2, slot_rows, piece + depth), BF16),
             pltpu.VMEM((PIECES - 1, n_grid, slot_rows, piece), BF16),
             pltpu.VMEM((n_grid, slot_rows, piece + depth), BF16),
             pltpu.VMEM((n_states, PIECES, atoms * nproj, piece), BF16),
@@ -480,7 +522,9 @@
             pltpu.VMEM((cells, depth), F32),
             pltpu.SemaphoreType.DMA((6,)),
             pltpu.SemaphoreType.DMA((PIECES, tiles, n_states)),
-            pltpu.SemaphoreType.DMA((PIECES, tiles, n_states)),
+            pltpu.SemaphoreType.DMA((PIECES, sides)),
+            pltpu.SemaphoreType.DMA((PIECES, sides)),
+            pltpu.SemaphoreType.DMA((PIECES, sides, tiles, 2)),
             pltpu.SemaphoreType.DMA((PIECES, n_grid)),
             pltpu.SemaphoreType.DMA((PIECES, n_states)),
             pltpu.SemaphoreType.DMA((PIECES, n_states)),

time: 39.4 us -> 37.3 us (0.947)
  Pallas kernels: 37.5 us -> 35.4 us
    pallas_call x1, Pallas kernels: 37.5 us -> 35.4 us  [shards(): pl.pallas_call(functools.partial(kernel, dims), out_shape=jax.ShapeDtypeS...]
where the time goes in v4:
time: 37.3 us; the launch traced here: 37 us
  Pallas kernels  35.4 us (95%)
  local copies, waits for them, and re-layouts  1.67 us (4%)
    pallas_call x1, Pallas kernels, shards(): pl.pallas_call(functools.partial(kernel, dims), out_shape=jax.ShapeDtypeS...  35.4 us
    unnamed x1, local copies, waits for them, and re-layouts  1.67 us

profile of v4, /device:TPU:0, one launch (start us, length us, event | category | flops | bytes accessed | tf_op | source)
XLA Modules:
  0.0 37.0 jit_solution(3685007519843339780)
XLA Ops:
  0.0 35.4 %shard_map.109 = f32[512,128]{1,0:T(8,128)} custom-call(f32[512,128]{1,0:T(8,128)} %bitcast.6, f32[512,128]{1,0:T(8,128)} %bitcast.7, bf16[32,4096]{1,0:T(8,128)(2,1)} %bitcast.8, bf16[512,512]{1,0:T(8,128)(2,1)} %constant.8.clone.inner_h_hbm, bf16[512,512]{1,0:T(8,128)(2,1)} %constant.9.clone.inner_l_hbm, bf16[2,2,192,192]{3,2,1,0:T(8,128)(2,1)} %constant.10.clone.rim_hbm, ...), custom_call_target="tpu_custom_call" | custom-call | flops 1157627904 | bytes 4194304 | tf_op jit(solution)/shard_map/pallas_call | solution.py:498
  35.4 1.7 %copy.13 = f32[1,16,32,128]{3,2,1,0:T(8,128)} copy(f32[1,16,32,128]{3,2,1,0:T(8,128)} %bitcast.5) | data formatting | bytes 524288

commit v5 on v4

--- a/solution.py
+++ b/solution.py
@@ -13,7 +13,7 @@
 RADIUS = 6
 PAIR_CAP = 2
 ATOM_PAD = 16
-PIECES = 2
+MOST_PIECES = 4
 
 MIXED_WEIGHT = 0.7
 CENTER = 12.0
@@ -134,7 +134,8 @@
     cells, depth = v_ref.shape
     breadth_bits, proj_bits = breadth.bit_length() - 1, nproj.bit_length() - 1
     rim = RADIUS * breadth
-    piece = chunk // PIECES
+    count = min(MOST_PIECES, chunk // depth)
+    piece = chunk // count
     blocks = piece // depth
     slot_rows = PAIR_CAP * nproj
     me_g, me_s = lax.axis_index("grid"), lax.axis_index("states")
@@ -153,13 +154,13 @@
         copy.wait_send()
 
     def outgoing(h, x):
-        return sendbuf_last.at[x] if h == PIECES - 1 else sendbuf.at[h, x]
+        return sendbuf_last.at[x] if h == count - 1 else sendbuf.at[h, x]
 
     def relayed(h, x):
-        return relay_last.at[x] if h == PIECES - 1 else relay.at[h, x]
+        return relay_last.at[x] if h == count - 1 else relay.at[h, x]
 
     def incoming(h, o):
-        return arrived_last.at[o] if h == PIECES - 1 else arrived.at[h, o]
+        return arrived_last.at[o] if h == count - 1 else arrived.at[h, o]
 
     piece_loads = [
         pltpu.make_async_copy(
@@ -167,7 +168,7 @@
             outgoing(h, s // 2).at[i, s % 2, :, pl.ds(0, piece)],
             piece_sem.at[h, i, s],
         )
-        for h in range(PIECES)
+        for h in range(count)
         for i in range(tiles)
         for s in range(n_states)
     ]
@@ -292,10 +293,18 @@
             device_id_type=MESH,
         )
 
-    for h in range(PIECES):
+    for h in range(count):
         for d in range(sides - 1):
             hop_copy(h, d).start()
-        part_copies(h, 0, start_copy)
+        if h < 2:
+            part_copies(h, 0, start_copy)
+
+    def forward_parts(h):
+        for d in range(sides - 1):
+            await_hop(h, d)
+            part_copies(h, d + 1, start_copy)
+        if h + 2 < count:
+            part_copies(h + 2, 0, start_copy)
 
     owners = [owner_ref[a] for a in range(atoms)]
     slots, ranks = [], []
@@ -325,6 +334,7 @@
         0.0,
     ).astype(BF16)
 
+    forward_parts(0)
     block_rows = rows_ref.shape[1]
     local = rows_ref[...] - me_g * cells
     local = jnp.concatenate(
@@ -336,13 +346,6 @@
     )
     pick_ref[...] = pick.astype(BF16)
 
-    for h in range(PIECES):
-        for d in range(sides - 1):
-            await_hop(h, d)
-            part_copies(h, d + 1, start_copy)
-    for copy in halo_copies(0):
-        copy.start()
-
 
     def own_cells(step, field):
         hi = hi_ref[step]
@@ -368,7 +371,7 @@
     def nonlocal_part(step, gains):
         picked = dot(pick_ref[...], hi_ref[step]).astype(BF16)
         coefficients = jnp.zeros((ATOM_PAD, atoms * nproj), F32)
-        pairs = [(q, h) for q in range(n_states) for h in range(PIECES)]
+        pairs = [(q, h) for q in range(n_states) for h in range(count)]
         for n, (q, h) in enumerate(pairs):
             lines = [
                 picked[b * ATOM_PAD : (b + 1) * ATOM_PAD]
@@ -408,16 +411,21 @@
                     device_id_type=MESH,
                 ).wait_recv()
 
-        last = h == PIECES - 1
+        last = h == count - 1
         came = arrived_last[:, :, :piece] if last else arrived[h]
         parts[me_s, h] = dot(chosen, came.reshape(width, piece)).astype(BF16)
         for index, s in enumerate(twins):
             share_copy(h, 1 + index, me_s, s).start()
         share_copy(h, 0, me_s, partner).start()
 
-    take_share(0)
+    for h in range(1, count):
+        forward_parts(h)
+        if h >= 2:
+            take_share(h - 2)
+    for copy in halo_copies(0):
+        copy.start()
     place_ref[...] = pick.T.astype(BF16)
-    for h in range(1, PIECES):
+    for h in range(max(count - 2, 0), count):
         take_share(h)
     load_pot.wait()
     for load in load_tables:
@@ -437,15 +445,15 @@
 
     base_ref[...] = (pot_ref[...] - CENTER) * (1.0 / HALF_WIDTH) + centre_weight
 
-    for h in range(PIECES - 1):
+    for h in range(count - 1):
         forward(h)
     start = v_ref[...]
     first = own_cells(0, start)
-    forward(PIECES - 1)
+    forward(count - 1)
     first = first + rims(0)
     gain_lines = arrived_last[:, :, piece:].reshape(width, depth)
     gains = dot(dot(slot_lines, gain_lines).astype(BF16), spread)
-    for h in range(PIECES):
+    for h in range(count):
         share_copy(h, 0, partner, partner).wait_recv()
         for s in twins:
             share_copy(h, 0, s + 1 - 2 * lax.rem(s, 2), partner).wait_recv()
@@ -462,7 +470,7 @@
     last = own_cells(2, second) + nonlocal_part(2, gains)
     out_ref[...] = 2.0 * (last + rims(2)) - first
 
-    for h in range(PIECES):
+    for h in range(count):
         for d in range(sides - 1):
             hop_copy(h, d).wait_send()
         for d in range(sides):
@@ -484,7 +492,8 @@
     cells, rim = planes * breadth, RADIUS * breadth
     tiles = held // PAIR_CAP
     chunk = span // n_states
-    piece, sides = chunk // PIECES, n_states // 2
+    count = min(MOST_PIECES, chunk // depth)
+    piece, sides = chunk // count, n_states // 2
     slot_rows = PAIR_CAP * nproj
     inner, low, high, across, centre_weight = stencil_matrices(planes, breadth, depth)
     inner_h, inner_l = halves(inner)
@@ -507,13 +516,13 @@
             pltpu.VMEM((cells, cells), BF16),
             pltpu.VMEM((2, 2, rim, rim), BF16),
             pltpu.VMEM((depth, 2 * depth), BF16),
-            pltpu.VMEM((PIECES - 1, sides, tiles, 2, slot_rows, piece), BF16),
+            pltpu.VMEM((count - 1, sides, tiles, 2, slot_rows, piece), BF16),
             pltpu.VMEM((sides, tiles, 2, slot_rows, piece + depth), BF16),
-            pltpu.VMEM((PIECES - 1, sides, tiles, 2, slot_rows, piece), BF16),
+            pltpu.VMEM((count - 1, sides, tiles, 2, slot_rows, piece), BF16),
             pltpu.VMEM((sides, tiles, 2, slot_rows, piece + depth), BF16),
-            pltpu.VMEM((PIECES - 1, n_grid, slot_rows, piece), BF16),
+            pltpu.VMEM((count - 1, n_grid, slot_rows, piece), BF16),
             pltpu.VMEM((n_grid, slot_rows, piece + depth), BF16),
-            pltpu.VMEM((n_states, PIECES, atoms * nproj, piece), BF16),
+            pltpu.VMEM((n_states, count, atoms * nproj, piece), BF16),
             pltpu.VMEM((3, cells, depth), BF16),
             pltpu.VMEM((3, 2, rim, depth), BF16),
             pltpu.VMEM((ATOM_PAD * atom_rows.shape[1], cells), BF16),
@@ -521,13 +530,13 @@
             pltpu.VMEM((2, 2, rim, rim), BF16),
             pltpu.VMEM((cells, depth), F32),
             pltpu.SemaphoreType.DMA((6,)),
-            pltpu.SemaphoreType.DMA((PIECES, tiles, n_states)),
-            pltpu.SemaphoreType.DMA((PIECES, sides)),
-            pltpu.SemaphoreType.DMA((PIECES, sides)),
-            pltpu.SemaphoreType.DMA((PIECES, sides, tiles, 2)),
-            pltpu.SemaphoreType.DMA((PIECES, n_grid)),
-            pltpu.SemaphoreType.DMA((PIECES, n_states)),
-            pltpu.SemaphoreType.DMA((PIECES, n_states)),
+            pltpu.SemaphoreType.DMA((count, tiles, n_states)),
+            pltpu.SemaphoreType.DMA((count, sides)),
+            pltpu.SemaphoreType.DMA((count, sides)),
+            pltpu.SemaphoreType.DMA((count, sides, tiles, 2)),
+            pltpu.SemaphoreType.DMA((count, n_grid)),
+            pltpu.SemaphoreType.DMA((count, n_states)),
+            pltpu.SemaphoreType.DMA((count, n_states)),
             pltpu.SemaphoreType.DMA((3, 2)),
             pltpu.SemaphoreType.DMA((3, 2)),
         ],

time: 37.3 us -> 36.8 us (0.987)
  Pallas kernels: 35.4 us -> 34.9 us
    pallas_call x1, Pallas kernels: 35.4 us -> 34.9 us  [shards(): pl.pallas_call(functools.partial(kernel, dims), out_shape=jax.ShapeDtypeS...]
where the time goes in v5:
time: 36.8 us; the launch traced here: 36.6 us
  Pallas kernels  34.9 us (95%)
  local copies, waits for them, and re-layouts  1.67 us (5%)
    pallas_call x1, Pallas kernels, shards(): pl.pallas_call(functools.partial(kernel, dims), out_shape=jax.ShapeDtypeS...  34.9 us
    unnamed x1, local copies, waits for them, and re-layouts  1.67 us

profile of v5, /device:TPU:0, one launch (start us, length us, event | category | flops | bytes accessed | tf_op | source)
XLA Modules:
  0.0 36.6 jit_solution(7054570956888320719)
XLA Ops:
  0.0 34.9 %shard_map.109 = f32[512,128]{1,0:T(8,128)} custom-call(f32[512,128]{1,0:T(8,128)} %bitcast.6, f32[512,128]{1,0:T(8,128)} %bitcast.7, bf16[32,4096]{1,0:T(8,128)(2,1)} %bitcast.8, bf16[512,512]{1,0:T(8,128)(2,1)} %constant.8.clone.inner_h_hbm, bf16[512,512]{1,0:T(8,128)(2,1)} %constant.9.clone.inner_l_hbm, bf16[2,2,192,192]{3,2,1,0:T(8,128)(2,1)} %constant.10.clone.rim_hbm, ...), custom_call_target="tpu_custom_call" | custom-call | flops 1157627904 | bytes 4194304 | tf_op jit(solution)/shard_map/pallas_call | solution.py:507
  34.9 1.7 %copy.13 = f32[1,16,32,128]{3,2,1,0:T(8,128)} copy(f32[1,16,32,128]{3,2,1,0:T(8,128)} %bitcast.5) | data formatting | bytes 524288

commit v6 on v5

--- a/solution.py
+++ b/solution.py
@@ -185,9 +185,9 @@
             )
         )
     ]
-    load_v.start()
     for load in piece_loads:
         load.start()
+    load_v.start()
     load_pot.start()
     for load in load_tables:
         load.start()
@@ -217,10 +217,6 @@
         block = jnp.concatenate([jnp.concatenate([own_rows, below], axis=0), nothing], axis=1)
         for s in range(n_states):
             sendbuf_last[s // 2, i, s % 2, :, piece:] = block
-    load_v.wait()
-    hi_ref[0] = v_ref[...].astype(BF16)
-    for load in piece_loads:
-        load.wait()
 
     pl.semaphore_wait(barrier, n_grid + 2 + len(twins) + jnp.where(source_s == me_s, 0, 1))
 
@@ -293,7 +289,10 @@
             device_id_type=MESH,
         )
 
+    per_piece = tiles * n_states
     for h in range(count):
+        for load in piece_loads[h * per_piece : (h + 1) * per_piece]:
+            load.wait()
         for d in range(sides - 1):
             hop_copy(h, d).start()
         if h < 2:
@@ -305,6 +304,9 @@
             part_copies(h, d + 1, start_copy)
         if h + 2 < count:
             part_copies(h + 2, 0, start_copy)
+
+    load_v.wait()
+    hi_ref[0] = v_ref[...].astype(BF16)
 
     owners = [owner_ref[a] for a in range(atoms)]
     slots, ranks = [], []
@@ -354,9 +356,8 @@
         wide = dot(inner_h_ref[...], both)
         total = base_ref[...] * field
         total = total + (wide[:, :depth] + wide[:, depth:] + dot(inner_l_ref[...], hi))
-        across = dot(hi, across_ref[...])
-        total = total + (across[:, :depth] + across[:, depth:])
-        return total + dot(lo, across_ref[:, :depth])
+        across = dot(both, across_ref[...])
+        return total + (across[:, :depth] + across[:, depth:])
 
     def rims(step):
         for copy in halo_copies(step):
@@ -370,7 +371,7 @@
 
     def nonlocal_part(step, gains):
         picked = dot(pick_ref[...], hi_ref[step]).astype(BF16)
-        coefficients = jnp.zeros((ATOM_PAD, atoms * nproj), F32)
+        coefficients = jnp.zeros((atoms * nproj, ATOM_PAD), F32)
         pairs = [(q, h) for q in range(n_states) for h in range(count)]
         for n, (q, h) in enumerate(pairs):
             lines = [
@@ -378,11 +379,12 @@
                 for b in range(n * blocks, (n + 1) * blocks)
             ]
             coefficients = coefficients + lax.dot_general(
+                parts[q, h],
                 jnp.concatenate(lines, axis=1),
-                parts[q, h],
                 (((1,), (1,)), ((), ())),
                 preferred_element_type=F32,
             )
+        coefficients = coefficients.T
         atom = lax.broadcasted_iota(jnp.int32, coefficients.shape, 0)
         column = lax.broadcasted_iota(jnp.int32, coefficients.shape, 1)
         scaled = jnp.where((column >> proj_bits) == atom, coefficients * gains, 0.0).astype(BF16)
@@ -468,7 +470,7 @@
     for copy in halo_copies(2):
         copy.start()
     last = own_cells(2, second) + nonlocal_part(2, gains)
-    out_ref[...] = 2.0 * (last + rims(2)) - first
+    out_ref[...] = (last + rims(2)) - 0.5 * first
 
     for h in range(count):
         for d in range(sides - 1):
@@ -498,7 +500,8 @@
     inner, low, high, across, centre_weight = stencil_matrices(planes, breadth, depth)
     inner_h, inner_l = halves(inner)
     rim_matrices = np.stack([np.stack(halves(low)), np.stack(halves(high))])
-    across_both = np.concatenate(halves(across), axis=1)
+    across_h, across_l = halves(across)
+    across_both = np.block([[across_h, across_l], [across_h, np.zeros_like(across_l)]])
     dims = (n_grid, n_states, tiles, chunk, breadth, nproj, atoms, centre_weight)
     hbm = pl.BlockSpec(memory_space=pltpu.HBM)
     vmem = pl.BlockSpec(memory_space=pltpu.VMEM)
@@ -515,7 +518,7 @@
             pltpu.VMEM((cells, cells), BF16),
             pltpu.VMEM((cells, cells), BF16),
             pltpu.VMEM((2, 2, rim, rim), BF16),
-            pltpu.VMEM((depth, 2 * depth), BF16),
+            pltpu.VMEM((2 * depth, 2 * depth), BF16),
             pltpu.VMEM((count - 1, sides, tiles, 2, slot_rows, piece), BF16),
             pltpu.VMEM((sides, tiles, 2, slot_rows, piece + depth), BF16),
             pltpu.VMEM((count - 1, sides, tiles, 2, slot_rows, piece), BF16),
@@ -559,7 +562,7 @@
         atom_rows,
         wrap_rows,
     )
-    return out.reshape(states_in.shape)
+    return 2.0 * out.reshape(states_in.shape)
 
 
 def solution(mesh):

time: 36.8 us -> 36.8 us (level)
  other arithmetic: 0 us -> 1.67 us
  local copies, waits for them, and re-layouts: 1.67 us -> 0 us
    mul x0 -> x1, other arithmetic: none -> 1.67 us  [shards(): return 2.0 * out.reshape(states_in.shape)]
    unnamed x1 -> x0, local copies, waits for them, and re-layouts: 1.67 us -> none
where the time goes in v6:
time: 36.8 us; the launch traced here: 36.7 us
  Pallas kernels  35 us (95%)
  other arithmetic  1.67 us (5%)
    pallas_call x1, Pallas kernels, shards(): pl.pallas_call(functools.partial(kernel, dims), out_shape=jax.ShapeDtypeS...  35 us
    mul x1, other arithmetic, shards(): return 2.0 * out.reshape(states_in.shape)  1.67 us

profile of v6, /device:TPU:0, one launch (start us, length us, event | category | flops | bytes accessed | tf_op | source)
XLA Modules:
  0.0 36.7 jit_solution(6185355744667541761)
XLA Ops:
  0.0 35.0 %shard_map.109 = f32[512,128]{1,0:T(8,128)} custom-call(f32[512,128]{1,0:T(8,128)} %bitcast.5, f32[512,128]{1,0:T(8,128)} %bitcast.6, bf16[32,4096]{1,0:T(8,128)(2,1)} %bitcast.7, bf16[512,512]{1,0:T(8,128)(2,1)} %constant.10.clone.inner_h_hbm, bf16[512,512]{1,0:T(8,128)(2,1)} %constant.11.clone.inner_l_hbm, ...), custom_call_target="tpu_custom_call" | custom-call | flops 1157627904 | bytes 4194304 | tf_op jit(solution)/shard_map/pallas_call | solution.py:510
  35.0 1.7 %broadcast_multiply_fusion = f32[512,128]{1,0:T(8,128)} fusion(f32[512,128]{1,0:T(8,128)} %shard_map.109), kind=kLoop, calls=%fused_computation | loop fusion | flops 65536 | bytes 524288 | tf_op jit(solution)/shard_map/mul | solution.py:565
